TPU v7x, 32 devices: a whole 2x2x4 slice. The times are simulated.
32 devices in a mesh: seq: 4 (over z), head: 4 (over y, x), dp: 2 (over core).
Axes of the slice: x: 2, y: 2, z: 4, core: 2. Of those that a mesh axis runs over, the one named last changes fastest.
Arguments:
- tokens: float32 [8, 784, 1024], P('dp', 'seq', 'head'), may hold values from -6 to 6
- gain_attn: float32 [1024], P('head'), may hold values from 0.5 to 1.5
- qkv_weight: float32 [1024, 3, 1024], P(None, None, 'head'), may hold values from -0.1875 to 0.1875
- out_weight: float32 [1024, 1024], P('head'), may hold values from -0.75 to 0.75
- gain_ffn: float32 [1024], P('head'), may hold values from 0.5 to 1.5
- up_weight: float32 [1024, 4096], P(None, 'head'), may hold values from -0.1875 to 0.1875
- up_bias: float32 [4096], P('head'), may hold values from -3 to 3
- down_weight: float32 [4096, 1024], P('head'), may hold values from -0.09375 to 0.09375
- down_bias: float32 [1024], P('head'), may hold values from -3 to 3
- out_grad: float32 [8, 784, 1024], P('dp', 'seq', 'head'), may hold values from -6 to 6
Outputs:
- output: float32 [8, 784, 1024], P('dp', 'seq', 'head')
- tokens_grad: float32 [8, 784, 1024], P('dp', 'seq', 'head')
- gain_attn_grad: float32 [1024], P('head')
- qkv_weight_grad: float32 [1024, 3, 1024], P(None, None, 'head')
- out_weight_grad: float32 [1024, 1024], P('head')
- gain_ffn_grad: float32 [1024], P('head')
- up_weight_grad: float32 [1024, 4096], P(None, 'head')
- up_bias_grad: float32 [4096], P('head')
- down_weight_grad: float32 [4096, 1024], P('head')
- down_bias_grad: float32 [1024], P('head')
All inputs are finite; a program needn't handle non-finite values.
Results may differ from a plain program's by a relative error of at most 0.0003.
Values sent between devices are 32-bit elements; how exact they have to be, the bound alone decides.
A program may use at most 192 MiB of HBM per device.

v0:
```python
import jax
import jax.numpy as jnp
from jax import lax
from jax.sharding import PartitionSpec as P

HEAD_DIM = 64


highest = lax.Precision.HIGHEST
norm_eps = 1e-05


def entering(part, axis, combine, identity, reverse):
    count = lax.axis_size(axis)
    place = lax.axis_index(axis)
    ahead = count - 1 - place if reverse else place
    gathered = jax.tree.map(lambda a: lax.all_gather(a, axis), part)
    state = jax.tree.map(lambda a, e: jnp.zeros_like(a) + jnp.asarray(e, a.dtype), part, identity)

    def one(turn, state):
        source = count - 1 - turn if reverse else turn
        return combine(
            state, jax.tree.map(lambda a: lax.dynamic_index_in_dim(a, source, 0, False), gathered)
        )

    return lax.fori_loop(0, ahead, one, state)


def feature(values_in):
    return jax.nn.elu(values_in) + 1.0


def layer_norm(values_in, gain):
    row_mean = jnp.mean(values_in, axis=-1, keepdims=True)
    centred = values_in - row_mean
    row_var = jnp.mean(centred * centred, axis=-1, keepdims=True)
    return centred * lax.rsqrt(row_var + norm_eps) * gain


def mlp_act(values_in):
    return jax.nn.gelu(values_in, approximate=True)


def block_attend(query_proj, key_proj, value_proj, prior_state, prior_total):
    query_feat = feature(query_proj)
    key_feat = feature(key_proj)
    length_now = query_proj.shape[1]
    scores = jnp.einsum("gihe,gjhe->ghij", query_feat, key_feat, precision=highest)
    row_index = lax.broadcasted_iota(jnp.int32, (length_now, length_now), 0)
    col_index = lax.broadcasted_iota(jnp.int32, (length_now, length_now), 1)
    scores = jnp.where(col_index <= row_index, scores, jnp.float32(0.0))
    numerator = jnp.einsum("ghij,gjhe->gihe", scores, value_proj, precision=highest)
    numerator = numerator + jnp.einsum(
        "gihe,ghef->gihf", query_feat, prior_state, precision=highest
    )
    denominator = jnp.sum(scores, axis=-1) + jnp.einsum(
        "gihe,ghe->ghi", query_feat, prior_total, precision=highest
    )
    return numerator / jnp.transpose(denominator, (0, 2, 1))[..., None]


def block_state(key_proj, value_proj):
    key_feat = feature(key_proj)
    kv_sum = jnp.einsum("gihe,gihf->ghef", key_feat, value_proj, precision=highest)
    return (kv_sum, jnp.sum(key_feat, axis=1))


def add_pair(earlier, later):
    return (earlier[0] + later[0], earlier[1] + later[1])


def per_device(
    tokens,
    gain_attn,
    qkv_weight,
    out_weight,
    gain_ffn,
    up_weight,
    up_bias,
    down_weight,
    down_bias,
    out_grad,
):
    image_count, block_len, local_width = tokens.shape
    row_count = image_count * block_len
    model_width = qkv_weight.shape[0]
    heads_local = local_width // HEAD_DIM
    column_start = lax.axis_index("head") * local_width
    full_tokens, gain_first, gain_second = (
        lax.all_gather(tokens, "head", axis=2, tiled=True),
        lax.all_gather(gain_attn, "head", axis=0, tiled=True),
        lax.all_gather(gain_ffn, "head", axis=0, tiled=True),
    )
    token_rows = full_tokens.reshape(row_count, model_width)
    normed_one, pull_one = jax.vjp(layer_norm, token_rows, gain_first)
    proj_weight = qkv_weight.reshape(model_width, 3 * local_width)
    projected = jnp.dot(normed_one, proj_weight, precision=highest)
    parts_view = projected.reshape(image_count, block_len, 3, heads_local, HEAD_DIM)
    query_proj = parts_view[:, :, 0]
    key_proj = parts_view[:, :, 1]
    value_proj = parts_view[:, :, 2]
    (own_state, own_total), pull_state = jax.vjp(block_state, key_proj, value_proj)
    zero_pair = (jnp.zeros_like(own_state), jnp.zeros_like(own_total))
    prior_state, prior_total = entering((own_state, own_total), "seq", add_pair, zero_pair, False)
    mixed, pull_attend = jax.vjp(
        block_attend, query_proj, key_proj, value_proj, prior_state, prior_total
    )
    mixed_rows = mixed.reshape(row_count, local_width)
    branch_out = jnp.dot(mixed_rows, out_weight, precision=highest)
    token_share = tokens.reshape(row_count, local_width)
    resid_share = token_share + lax.psum_scatter(
        branch_out, "head", scatter_dimension=1, tiled=True
    )
    resid_full = lax.all_gather(resid_share, "head", axis=1, tiled=True)
    normed_two, pull_two = jax.vjp(layer_norm, resid_full, gain_second)
    up_proj = jnp.dot(normed_two, up_weight, precision=highest) + up_bias
    hidden, pull_act = jax.vjp(mlp_act, up_proj)
    down_proj = jnp.dot(hidden, down_weight, precision=highest)
    ffn_share = lax.psum_scatter(down_proj, "head", scatter_dimension=1, tiled=True)
    output = (resid_share + ffn_share + down_bias).reshape(tokens.shape)
    grad_share = out_grad.reshape(row_count, local_width)
    grad_full = lax.all_gather(grad_share, "head", axis=1, tiled=True)
    down_bias_grad = jnp.sum(grad_share, axis=0)
    down_weight_grad = jnp.dot(hidden.T, grad_full, precision=highest)
    hidden_grad = jnp.dot(grad_full, down_weight.T, precision=highest)
    (up_grad,) = pull_act(hidden_grad)
    up_bias_grad = jnp.sum(up_grad, axis=0)
    up_weight_grad = jnp.dot(normed_two.T, up_grad, precision=highest)
    normed_two_grad = lax.psum(jnp.dot(up_grad, up_weight.T, precision=highest), "head")
    resid_back, gain_second_grad = pull_two(normed_two_grad)
    resid_grad = grad_full + resid_back
    out_weight_grad = jnp.dot(mixed_rows.T, resid_grad, precision=highest)
    mixed_grad = jnp.dot(resid_grad, out_weight.T, precision=highest).reshape(mixed.shape)
    query_grad, key_grad, value_grad, state_grad, total_grad = pull_attend(mixed_grad)
    later_state, later_total = entering((state_grad, total_grad), "seq", add_pair, zero_pair, True)
    key_extra, value_extra = pull_state((later_state, later_total))
    key_grad = key_grad + key_extra
    value_grad = value_grad + value_extra
    proj_grad = jnp.stack([query_grad, key_grad, value_grad], axis=2).reshape(
        row_count, 3 * local_width
    )
    qkv_weight_grad = jnp.dot(normed_one.T, proj_grad, precision=highest).reshape(qkv_weight.shape)
    normed_one_grad = lax.psum(jnp.dot(proj_grad, proj_weight.T, precision=highest), "head")
    token_back, gain_first_grad = pull_one(normed_one_grad)
    tokens_full_grad = resid_grad + token_back
    tokens_grad = lax.dynamic_slice_in_dim(tokens_full_grad, column_start, local_width, 1).reshape(
        tokens.shape
    )
    gain_attn_share = lax.dynamic_slice_in_dim(gain_first_grad, column_start, local_width, 0)
    gain_ffn_share = lax.dynamic_slice_in_dim(gain_second_grad, column_start, local_width, 0)
    summed_grads = lax.psum(
        (
            gain_attn_share,
            qkv_weight_grad,
            out_weight_grad,
            gain_ffn_share,
            up_weight_grad,
            up_bias_grad,
            down_weight_grad,
            down_bias_grad,
        ),
        ("seq", "dp"),
    )
    return (
        output,
        tokens_grad,
        summed_grads[0],
        summed_grads[1],
        summed_grads[2],
        summed_grads[3],
        summed_grads[4],
        summed_grads[5],
        summed_grads[6],
        summed_grads[7],
    )


def solution(mesh):
    return jax.shard_map(
        per_device,
        mesh=mesh,
        in_specs=(
            P("dp", "seq", "head"),
            P("head"),
            P(None, None, "head"),
            P("head", None),
            P("head"),
            P(None, "head"),
            P("head"),
            P("head", None),
            P("head"),
            P("dp", "seq", "head"),
        ),
        out_specs=(
            P("dp", "seq", "head"),
            P("dp", "seq", "head"),
            P("head"),
            P(None, None, "head"),
            P("head", None),
            P("head"),
            P(None, "head"),
            P("head"),
            P("head", None),
            P("head"),
        ),
        check_vma=False,
    )
```

profile of v0, /device:TPU:0, one launch (start us, length us, event | category | flops | bytes accessed | tf_op | source)
XLA Modules:
  0.0 885.8 jit_solution(9425930872226420117)
XLA Ops:
  8.0 3.5 copy.86
  11.5 9.5 %all-gather.4 = f32[4,1,256]{2,1,0:T(1,128)S(1)} all-gather(f32[1,1,256]{2,1,0:T(1,128)S(1)} %bitcast.168), channel_id=1, replica_groups=mesh['seq'=4,'head'=4,'dp'=2] {'head'}, dimensions={0}, use_global_device_ids=true | all-gather | bytes 5120 | tf_op jit(solution)/shard_map/all_gather | solution.py:91
  21.0 35.9 %all-gather.12.cloned.1.call-done = f32[4,196,1024]{2,0,1:T(4,128)} async-done(((f32[4,196,256]{2,0,1:T(4,128)}), f32[4,196,1024]{2,0,1:T(4,128)}) %all-gather.12.cloned.1.call-update) | async-done | bytes 3211280 | tf_op jit(solution)/shard_map/all_gather | solution.py:90
  57.0 2.4 reduce_sum.132
  59.4 2.9 multiply_reduce_fusion.5
  63.2 2.8 fusion.134
  66.1 11.6 %fusion = f32[4,196,3,4,64]{1,4,3,2,0:T(8,128)S(1)} fusion(f32[3,4,64,1024,1]{3,2,1,0,4:T(8,128)S(1)} %bitcast.154, f32[4,196,1024,1,1]{2,0,1,4,3:T(4,128)S(1)} %fusion.134), kind=kOutput, calls=%fused_computation.8 | convolution fusion | flops 7398752256 | bytes 8765440 | tf_op jit(solution)/shard_map/dot_general | solution.py:97
  77.7 1.6 copy-done.7
  79.3 2.7 fusion.66
  82.1 1.8 fusion.87
  83.9 13.3 %all-gather.1 = f32[16,4,64]{2,1,0:T(4,128)S(1)} all-gather(f32[4,4,64]{2,1,0:T(4,128)S(1)} %fusion.87), channel_id=3, replica_groups=mesh['seq'=4,'head'=4,'dp'=2] {'seq'}, dimensions={0}, use_global_device_ids=true | all-gather | bytes 20480 | tf_op jit(solution)/shard_map/all_gather | solution.py:17
  97.3 7.0 select_reduce_fusion
  104.3 24.2 %all-gather.18.cloned.1.call-done = f32[16,4,64,64]{3,2,1,0:T(8,128)} async-done(((f32[4,4,64,64]{3,2,1,0:T(8,128)}), f32[16,4,64,64]{3,2,1,0:T(8,128)}) %all-gather.18.cloned.1.call-update) | async-done | bytes 1048592 | tf_op jit(solution)/shard_map/all_gather | solution.py:17
  128.6 2.4 fusion.94
  131.1 2.6 fusion.96
  134.3 4.7 broadcast_divide_fusion
  140.4 4.4 fusion.104
  147.1 44.4 %reduce-scatter.3.cloned.1.call-done = f32[784,256]{1,0:T(8,128)} async-done(((f32[784,1024]{1,0:T(8,128)}), f32[784,256]{1,0:T(8,128)}) %reduce-scatter.3.cloned.1.call-update) | async-done | bytes 802832 | tf_op jit(solution)/shard_map/reduce_scatter | solution.py:111
  191.6 2.4 add.166
  196.4 8.1 all-gather.5
  204.5 34.0 %all-gather.14.cloned.1.call-done = f32[784,1024]{1,0:T(8,128)} async-done(((f32[784,256]{1,0:T(8,128)}), f32[784,1024]{1,0:T(8,128)}) %all-gather.14.cloned.1.call-update) | async-done | bytes 3211280 | tf_op jit(solution)/shard_map/all_gather | solution.py:114
  238.5 2.1 reduce_sum.139
  240.7 2.5 multiply_reduce_fusion.4
  243.5 13.7 %fusion.10 = f32[784,1024]{1,0:T(8,128)} fusion(f32[1024,1024]{1,0:T(8,128)} %param.19, f32[784,1024]{1,0:T(8,128)S(1)} %copy-done.2, f32[1024]{0:T(1024)S(1)} %bitcast.163, f32[784]{0:T(1024)S(1)} %fusion.70, f32[784]{0:T(1024)S(1)} %broadcast_multiply_fusion.1), kind=kOutput, calls=%fused_computation.29 | convolution fusion | flops 9867411456 | bytes 10627200 | tf_op jit(solution)/shard_map/dot_general | solution.py:116
  257.2 27.9 %all-gather.16.cloned.1.call-done = f32[784,1024]{1,0:T(8,128)} async-done(((f32[784,256]{1,0:T(8,128)}), f32[784,1024]{1,0:T(8,128)}) %all-gather.16.cloned.1.call-update) | async-done | bytes 3211280 | tf_op jit(solution)/shard_map/all_gather | solution.py:122
  285.2 17.3 %fusion.99 = (f32[1024]{0:T(1024)}, f32[784,1024]{1,0:T(8,128)S(1)}) fusion(f32[784,1024]{1,0:T(8,128)} %fusion.10, f32[1024]{0:T(1024)S(1)} %copy-done.44, f32[784,1024]{1,0:T(8,128)} %all-gather.16.cloned.1.call-done, f32[1024,1024]{1,0:T(8,128)} %param.21), kind=kOutput, calls=%fused_computation.131 | convolution fusion | flops 9881861120 | bytes 13836288 | tf_op jit(solution)/shard_map/dot_general | solution.py:125
  302.5 1.7 copy-done.47
  304.2 12.1 %fusion.105 = f32[784,1024]{1,0:T(8,128)} fusion(f32[784,1024]{1,0:T(8,128)S(1)} %get-tuple-element.206, f32[1024,1024]{1,0:T(8,128)S(1)} %copy-done.43), kind=kOutput, calls=%fused_computation.135 | convolution fusion | flops 9865003008 | bytes 10616832 | tf_op jit(solution)/shard_map/dot_general | solution.py:129
  316.5 88.3 %all-reduce.6.cloned.1.call-done = f32[784,1024]{1,0:T(8,128)} async-done(((f32[784,1024]{1,0:T(8,128)}), f32[784,1024]{1,0:T(8,128)}) %all-reduce.6.cloned.1.call-update) | async-done | bytes 3211280 | tf_op jit(solution)/shard_map/psum | solution.py:129
  404.7 4.6 multiply_reduce_fusion
  411.8 1.7 copy-done.4
  413.5 4.6 fusion.106
  418.0 2.0 reshape.176
  420.1 3.6 fusion.57
  423.8 17.3 %fusion.55 = f32[784,1024]{1,0:T(8,128)} fusion(f32[1024,1024]{1,0:T(8,128)} %param.21, f32[784,1024]{1,0:T(8,128)} %fusion.10, f32[1024]{0:T(1024)S(1)} %copy-done.45), kind=kOutput, calls=%fused_computation.69 | convolution fusion | flops 9872228352 | bytes 10620928 | tf_op jit(solution)/shard_map/dot_general | solution.py:118
  443.4 2.7 fusion.68
  446.1 13.8 %all-gather.3 = f32[16,4,64]{2,1,0:T(4,128)S(1)} all-gather(f32[4,4,64]{2,1,0:T(4,128)S(1)} %bitcast.167), channel_id=5, replica_groups=mesh['seq'=4,'head'=4,'dp'=2] {'seq'}, dimensions={0}, use_global_device_ids=true | all-gather | bytes 20480 | tf_op jit(solution)/shard_map/all_gather | solution.py:17
  461.2 2.8 fusion.59
  464.1 5.1 fusion.52
  469.2 4.7 add_bitcast_fusion.1
  473.9 3.8 while.27
  477.7 2.9 fusion.84
  480.7 3.5 add_bitcast_fusion
  484.2 3.6 fusion.47
  488.2 3.7 copy.101
  491.9 5.0 reshape.177
  496.9 13.3 %fusion.107 = f32[784,1024]{1,0:T(8,128)} fusion(f32[784,768]{0,1:T(8,128)} %reshape.177, f32[1024,768]{0,1:T(8,128)} %bitcast.153), kind=kOutput, calls=%fused_computation.137 | convolution fusion | flops 7398752256 | bytes 8765440 | tf_op jit(solution)/shard_map/dot_general | solution.py:143
  511.1 2.7 multiply_multiply_fusion.2
  513.8 3.6 copy.103
  517.4 3.4 reshape.194
  520.8 18.0 %fusion.8 = f32[1024,1024]{1,0:T(8,128)} fusion(f32[784,1024]{1,0:T(8,128)} %copy-done.47, f32[784,1024]{1,0:T(8,128)} %all-gather.14.cloned.1.call-done, f32[1024]{0:T(1024)S(1)} %bitcast.166, f32[784]{0:T(1024)S(1)} %copy-done.37, f32[784]{0:T(1024)S(1)} %broadcast_multiply_fusion.1), kind=kOutput, calls=%fused_computation.27 | convolution fusion | flops 9867411456 | bytes 10627200 | tf_op jit(solution)/shard_map/dot_general | solution.py:128
  538.7 16.9 %fusion.54 = f32[1024,1024]{1,0:T(8,128)} fusion(f32[784,1024]{1,0:T(8,128)S(1)} %copy-done.18, f32[784,1024]{1,0:T(8,128)S(1)} %copy-done.48, f32[1024]{0:T(1024)S(1)} %copy-done.46), kind=kOutput, calls=%fused_computation.68 | convolution fusion | flops 9872228352 | bytes 10620928 | tf_op jit(solution)/shard_map/dot_general | solution.py:124
  555.7 4.6 fusion.109
  560.3 19.7 %fusion.108 = f32[1024,3,256]{2,0,1:T(8,128)} fusion(f32[784,1024,1]{1,0,2:T(8,128)S(1)} %copy-done.19, f32[3,256,784]{2,1,0:T(8,128)S(1)} %bitcast.155), kind=kOutput, calls=%fused_computation.138 | convolution fusion | flops 7398752256 | bytes 8765440 | tf_op jit(solution)/shard_map/dot_general | solution.py:142
  581.5 5.5 copy.102
  587.0 4.0 reshape.178
  594.5 13.6 %all-reduce.8.cloned.1.call-done = f32[784,1024]{1,0:T(8,128)} async-done(((f32[784,1024]{1,0:T(8,128)}), f32[784,1024]{1,0:T(8,128)}) %all-reduce.8.cloned.1.call-update) | async-done | bytes 3211280 | tf_op jit(solution)/shard_map/psum | solution.py:143
  608.1 4.0 multiply_reduce_fusion.1
  616.6 17.8 %all-reduce = (f32[256]{0:T(256)}, f32[256]{0:T(256)}, f32[1024]{0:T(1024)}, f32[256]{0:T(256)}) all-reduce(f32[256]{0:T(256)S(1)} %dynamic_slice.32, f32[256]{0:T(256)S(1)} %dynamic_slice.33, f32[1024]{0:T(1024)S(1)} %copy-done.39, f32[256]{0:T(256)S(1)} %reduce_sum.177), channel_id=1, replica_groups=mesh['seq'=4,'head'=4,'dp'=2] {'seq','dp'}, use_global_device_ids=true, to_apply=%region_20.21 | all-reduce | flops 1792 | bytes 14336 | tf_op jit(solution)/shard_map/psum | solution.py:151
  634.4 233.7 %all-reduce.10.cloned.1.call-done = (f32[1024,3,256]{2,0,1:T(8,128)}, f32[256,1024]{1,0:T(8,128)}, f32[1024,1024]{1,0:T(8,128)}, f32[1024,1024]{1,0:T(8,128)}) async-done(((f32[1024,3,256]{2,0,1:T(8,128)}, f32[256,1024]{1,0:T(8,128)}, f32[1024,1024]{1,0:T(8,128)}, f32[1024,1024]{1,0:T(8,128)}), (f32[1024,3,256]{2,0,1:T(8,128)}, f32[256,1024]{1,0:T(8,128)}, f32[1024,1024]{1,0:T(8,128)}, ...) | async-done | bytes 12582928 | tf_op jit(solution)/shard_map/psum | solution.py:151
  868.1 3.9 copy.172
  873.0 2.1 copy.174
  875.1 1.6 copy-done.14
  876.7 2.0 copy.175
  (166 shorter events, 30.3 us)
Async XLA Ops:
  7.2 133.2 %copy-start = (f32[256,1024]{1,0:T(8,128)S(1)}, f32[256,1024]{1,0:T(8,128)}, u32[]{:S(2)}) copy-start(f32[256,1024]{1,0:T(8,128)} %param.17) | copy-start | bytes 3145732
  7.2 49.8 %all-gather.12.cloned.1.call-start = ((), (), s32[]{:S(2)}) async-start(), calls=%async_computation.2 | async-start | bytes 4014080 | tf_op jit(solution)/shard_map/all_gather | solution.py:90
  7.9 3.6 copy-start.41
  7.9 120.6 %all-gather.18.cloned.1.call-start = ((), (), s32[]{:S(2)}) async-start(), calls=%async_computation.9 | async-start | bytes 2621440 | tf_op jit(solution)/shard_map/all_gather | solution.py:17
  59.4 6.6 copy-start.23
  63.1 2.9 copy-start.27
  63.2 2.9 copy-start.21
  77.7 1.6 copy-start.7
  82.0 109.6 %reduce-scatter.3.cloned.1.call-start = ((), (), s32[]{:S(2)}) async-start(), calls=%async_computation.3 | async-start | bytes 4014080 | tf_op jit(solution)/shard_map/reduce_scatter | solution.py:111
  82.1 52.2 %copy-start.29 = (pred[196,196]{0,1:T(8,128)(4,1)}, pred[196,196]{0,1:T(8,128)(4,1)S(1)}, u32[]{:S(2)}) copy-start(pred[196,196]{0,1:T(8,128)(4,1)S(1)} %iota_compare_fusion) | copy-start | bytes 115252
  128.6 5.7 copy-start.9
  134.3 4.7 copy-start.31
  144.8 93.7 %all-gather.14.cloned.1.call-start = ((), (), s32[]{:S(2)}) async-start(), calls=%async_computation.4 | async-start | bytes 4014080 | tf_op jit(solution)/shard_map/all_gather | solution.py:114
  147.1 49.2 %copy-start.42 = (f32[256]{0:T(256)S(1)}, f32[256]{0:T(256)}, u32[]{:S(2)}) copy-start(f32[256]{0:T(256)} %param.18) | copy-start | bytes 3076
  194.0 91.2 %all-gather.16.cloned.1.call-start = ((), (), s32[]{:S(2)}) async-start(), calls=%async_computation.6 | async-start | bytes 4014080 | tf_op jit(solution)/shard_map/all_gather | solution.py:122
  196.3 208.4 %all-reduce.6.cloned.1.call-start = ((), (), s32[]{:S(2)}) async-start(), calls=%async_computation.7 | async-start | bytes 6422528 | tf_op jit(solution)/shard_map/psum | solution.py:129
  204.5 204.9 %copy-start.34 = (f32[4,1,256]{2,1,0:T(1,128)}, f32[4,1,256]{2,1,0:T(1,128)S(1)}, u32[]{:S(2)}) copy-start(f32[4,1,256]{2,1,0:T(1,128)S(1)} %all-gather.5) | copy-start | bytes 12292
  240.6 2.9 copy-start.2
  243.2 166.2 %copy-start.36 = (f32[784]{0:T(1024)}, f32[784]{0:T(1024)S(1)}, u32[]{:S(2)}) copy-start(f32[784]{0:T(1024)S(1)} %fusion.70) | copy-start | bytes 9412
  243.5 41.6 %copy-start.44 = (f32[1024]{0:T(1024)S(1)}, f32[1024]{0:T(1024)}, u32[]{:S(2)}) copy-start(f32[1024]{0:T(1024)} %param.20) | copy-start | bytes 12292
  285.2 19.0 %copy-start.43 = (f32[1024,1024]{1,0:T(8,128)S(1)}, f32[1024,1024]{1,0:T(8,128)}, u32[]{:S(2)}) copy-start(f32[1024,1024]{1,0:T(8,128)} %param.19) | copy-start | bytes 12582916
  302.5 1.7 copy-start.47
  316.2 157.6 %all-gather.20.cloned.1.call-start = ((), (), s32[]{:S(2)}) async-start(), calls=%async_computation.10 | async-start | bytes 2621440 | tf_op jit(solution)/shard_map/all_gather | solution.py:17
  404.7 4.6 copy-start.3
  404.7 4.8 copy-start.12
  409.5 1.9 copy-start.17
  411.8 1.7 copy-start.4
  420.1 3.7 copy-start.45
  423.8 168.2 %reduce-scatter.5.cloned.1.call-start = ((), (), s32[]{:S(2)}) async-start(), calls=%async_computation.5 | async-start | bytes 4014080 | tf_op jit(solution)/shard_map/reduce_scatter | solution.py:119
  441.2 1.2 copy-start.16
  441.2 166.9 %all-reduce.8.cloned.1.call-start = ((), (), s32[]{:S(2)}) async-start(), calls=%async_computation.8 | async-start | bytes 6422528 | tf_op jit(solution)/shard_map/psum | solution.py:143
  441.2 18.7 %copy-start.32 = (f32[4,196,4]{1,2,0:T(4,128)S(1)}, f32[4,196,4]{1,2,0:T(4,128)}, u32[]{:S(2)}) copy-start(f32[4,196,4]{1,2,0:T(4,128)} %copy-done.31) | copy-start | bytes 37636
  443.4 17.8 %copy-start.8 = (f32[4,196,3,4,64]{1,4,3,2,0:T(8,128)S(1)}, f32[4,196,3,4,64]{1,4,3,2,0:T(8,128)}, u32[]{:S(2)}) copy-start(f32[4,196,3,4,64]{1,4,3,2,0:T(8,128)} %copy-done.7) | copy-start | bytes 7225348
  461.2 2.9 copy-start.30
  480.7 3.5 copy-start.10
  480.7 3.5 copy-start.33
  484.2 3.6 copy-start.26
  510.1 0.9 copy-start.24
  510.2 0.9 copy-start.28
  510.2 357.9 %all-reduce.10.cloned.1.call-start = ((), (), s32[]{:S(2)}) async-start(), calls=%async_computation.11 | async-start | bytes 25165824 | tf_op jit(solution)/shard_map/psum | solution.py:151
  517.4 3.4 copy-start.35
  517.4 3.4 copy-start.37
  520.7 18.0 %copy-start.18 = (f32[784,1024]{1,0:T(8,128)S(1)}, f32[784,1024]{1,0:T(8,128)}, u32[]{:S(2)}) copy-start(f32[784,1024]{1,0:T(8,128)} %all-gather.16.cloned.1.call-done) | copy-start | bytes 9633796
  520.7 18.0 %copy-start.46 = (f32[1024]{0:T(1024)S(1)}, f32[1024]{0:T(1024)}, u32[]{:S(2)}) copy-start(f32[1024]{0:T(1024)} %param.20) | copy-start | bytes 12292
  520.8 18.0 %copy-start.48 = (f32[784,1024]{1,0:T(8,128)S(1)}, f32[784,1024]{1,0:T(8,128)}, u32[]{:S(2)}) copy-start(f32[784,1024]{1,0:T(8,128)} %fusion.10) | copy-start | bytes 9633796
  538.7 16.9 %copy-start.5 = (f32[784,1024]{1,0:T(8,128)S(1)}, f32[784,1024]{1,0:T(8,128)}, u32[]{:S(2)}) copy-start(f32[784,1024]{1,0:T(8,128)} %copy-done.4) | copy-start | bytes 9633796
  538.7 21.6 %copy-start.22 = (f32[784,768]{0,1:T(8,128)S(1)}, f32[784,768]{0,1:T(8,128)}, u32[]{:S(2)}) copy-start(f32[784,768]{0,1:T(8,128)} %reshape.177) | copy-start | bytes 7225348
  555.7 4.6 copy-start.19
  580.1 1.1 copy-start.20
  587.0 4.1 copy-start.38
  587.0 5.0 copy-start.13
  587.0 5.0 copy-start.40
  608.1 4.0 copy-start.6
  608.1 4.8 copy-start.11
  613.9 2.7 copy-start.39
  868.1 3.9 copy-start.25
  868.1 4.9 copy-start.15
  873.0 3.7 copy-start.14
  873.0 5.7 copy-start.1
Sparse Core Ops, SparseCore 0:
  9.9 47.0 all-gather.11
  82.1 46.3 all-gather.17
  145.0 46.5 reduce-scatter.2
  194.1 44.3 all-gather.13
  240.7 44.3 all-gather.15
  316.4 88.3 all-reduce.5
  423.9 46.3 all-gather.19
  473.3 43.2 reduce-scatter.4
  519.8 88.3 all-reduce.7
  611.7 256.2 all-reduce.9
where the time goes:
time: 890 us; the launch traced here: 886 us
  waiting for transfers between devices  503 us (57%)
  matrix products  203 us (23%)
  blocking collectives  62.6 us (7%)
  local copies, waits for them, and re-layouts  61.5 us (7%)
  other arithmetic  39.7 us (4%)
  between operations  15.1 us (2%)
    psum x1, waiting for transfers between devices, per_device(): lax.psum((gain_attn_share, qkv_weight_grad, out_weight_grad, gain_ffn_sha...  234 us
    psum x1, waiting for transfers between devices, per_device(): lax.psum(jnp.dot(up_grad, up_weight.T, precision=highest), 'head')  88.3 us
    reduce_scatter x1, waiting for transfers between devices, per_device(): lax.psum_scatter(branch_out, 'head', scatter_dimension=1, tiled=True)  44.4 us
    all_gather x1, waiting for transfers between devices, per_device(): lax.all_gather(tokens, 'head', axis=2, tiled=True)  35.9 us
    all_gather x1, waiting for transfers between devices, per_device(): resid_full = lax.all_gather(resid_share, 'head', axis=1, tiled=True)  34 us
    unnamed x108, local copies, waits for them, and re-layouts  29.6 us
    all_gather x1, waiting for transfers between devices, per_device(): grad_full = lax.all_gather(grad_share, 'head', axis=1, tiled=True)  27.9 us
    all_gather x2, blocking collectives, entering(): gathered = jax.tree.map(lambda a: lax.all_gather(a, axis), part)  27.2 us
  transfers between devices with their start and end apart: 10, of which 8 were waited for; matrix products, arithmetic and copies ran while one was open for 22% of the time, Pallas kernels for 0%

commit v1 on v0

--- a/solution.py
+++ b/solution.py
@@ -6,7 +6,7 @@
 HEAD_DIM = 64
 
 
-highest = lax.Precision.HIGHEST
+highest = lax.Precision.HIGH
 norm_eps = 1e-05
 
 
@@ -35,6 +35,27 @@
     centred = values_in - row_mean
     row_var = jnp.mean(centred * centred, axis=-1, keepdims=True)
     return centred * lax.rsqrt(row_var + norm_eps) * gain
+
+
+def norm_back(partial_grad, rows_full, gain_full, gain_share):
+    local_width = gain_share.shape[0]
+    model_width = gain_full.shape[0]
+    row_mean = jnp.mean(rows_full, axis=-1, keepdims=True)
+    centred = rows_full - row_mean
+    row_inv = lax.rsqrt(jnp.mean(centred * centred, axis=-1, keepdims=True) + norm_eps)
+    scaled = partial_grad * gain_full
+    sums = lax.psum(
+        jnp.stack(
+            [jnp.sum(scaled, axis=-1), jnp.sum(scaled * (centred * row_inv), axis=-1)]
+        ),
+        "head",
+    )
+    means = (sums / model_width)[:, :, None]
+    share = lax.psum_scatter(partial_grad, "head", scatter_dimension=1, tiled=True)
+    start = lax.axis_index("head") * local_width
+    xhat = lax.dynamic_slice_in_dim(centred, start, local_width, 1) * row_inv
+    back = (share * gain_share - means[0] - xhat * means[1]) * row_inv
+    return back, jnp.sum(share * xhat, axis=0)
 
 
 def mlp_act(values_in):
@@ -92,7 +113,7 @@
         lax.all_gather(gain_ffn, "head", axis=0, tiled=True),
     )
     token_rows = full_tokens.reshape(row_count, model_width)
-    normed_one, pull_one = jax.vjp(layer_norm, token_rows, gain_first)
+    normed_one = layer_norm(token_rows, gain_first)
     proj_weight = qkv_weight.reshape(model_width, 3 * local_width)
     projected = jnp.dot(normed_one, proj_weight, precision=highest)
     parts_view = projected.reshape(image_count, block_len, 3, heads_local, HEAD_DIM)
@@ -112,7 +133,7 @@
         branch_out, "head", scatter_dimension=1, tiled=True
     )
     resid_full = lax.all_gather(resid_share, "head", axis=1, tiled=True)
-    normed_two, pull_two = jax.vjp(layer_norm, resid_full, gain_second)
+    normed_two = layer_norm(resid_full, gain_second)
     up_proj = jnp.dot(normed_two, up_weight, precision=highest) + up_bias
     hidden, pull_act = jax.vjp(mlp_act, up_proj)
     down_proj = jnp.dot(hidden, down_weight, precision=highest)
@@ -126,9 +147,12 @@
     (up_grad,) = pull_act(hidden_grad)
     up_bias_grad = jnp.sum(up_grad, axis=0)
     up_weight_grad = jnp.dot(normed_two.T, up_grad, precision=highest)
-    normed_two_grad = lax.psum(jnp.dot(up_grad, up_weight.T, precision=highest), "head")
-    resid_back, gain_second_grad = pull_two(normed_two_grad)
-    resid_grad = grad_full + resid_back
+    ffn_grads = lax.psum((up_weight_grad, down_weight_grad), ("seq", "dp"))
+    resid_back, gain_ffn_share = norm_back(
+        jnp.dot(up_grad, up_weight.T, precision=highest), resid_full, gain_second, gain_ffn
+    )
+    resid_grad_share = grad_share + resid_back
+    resid_grad = lax.all_gather(resid_grad_share, "head", axis=1, tiled=True)
     out_weight_grad = jnp.dot(mixed_rows.T, resid_grad, precision=highest)
     mixed_grad = jnp.dot(resid_grad, out_weight.T, precision=highest).reshape(mixed.shape)
     query_grad, key_grad, value_grad, state_grad, total_grad = pull_attend(mixed_grad)
@@ -140,23 +164,17 @@
         row_count, 3 * local_width
     )
     qkv_weight_grad = jnp.dot(normed_one.T, proj_grad, precision=highest).reshape(qkv_weight.shape)
-    normed_one_grad = lax.psum(jnp.dot(proj_grad, proj_weight.T, precision=highest), "head")
-    token_back, gain_first_grad = pull_one(normed_one_grad)
-    tokens_full_grad = resid_grad + token_back
-    tokens_grad = lax.dynamic_slice_in_dim(tokens_full_grad, column_start, local_width, 1).reshape(
-        tokens.shape
-    )
-    gain_attn_share = lax.dynamic_slice_in_dim(gain_first_grad, column_start, local_width, 0)
-    gain_ffn_share = lax.dynamic_slice_in_dim(gain_second_grad, column_start, local_width, 0)
+    token_back, gain_attn_share = norm_back(
+        jnp.dot(proj_grad, proj_weight.T, precision=highest), token_rows, gain_first, gain_attn
+    )
+    tokens_grad = (resid_grad_share + token_back).reshape(tokens.shape)
     summed_grads = lax.psum(
         (
             gain_attn_share,
             qkv_weight_grad,
             out_weight_grad,
             gain_ffn_share,
-            up_weight_grad,
             up_bias_grad,
-            down_weight_grad,
             down_bias_grad,
         ),
         ("seq", "dp"),
@@ -168,10 +186,10 @@
         summed_grads[1],
         summed_grads[2],
         summed_grads[3],
+        ffn_grads[0],
         summed_grads[4],
+        ffn_grads[1],
         summed_grads[5],
-        summed_grads[6],
-        summed_grads[7],
     )
 
 

time: 890 us -> 819 us (0.920)
  matrix products: 203 us -> 129 us
  blocking collectives: 62.6 us -> 92.6 us
  waiting for transfers between devices: 503 us -> 483 us
    psum x2 -> x0, waiting for transfers between devices: 102 us -> none  [the longest x1 88.3 us: per_device(): lax.psum(jnp.dot(up_grad, up_weight.T, precision=highest), 'head')]
    all_gather x0 -> x1, waiting for transfers between devices: none -> 44.1 us  [per_device(): resid_grad = lax.all_gather(resid_grad_share, 'head', axis=1, tiled=True)]
    reduce_scatter x0 -> x2, waiting for transfers between devices: none -> 36.1 us  [norm_back(): lax.psum_scatter(partial_grad, 'head', scatter_dimension=1, tiled=True)]
    psum x0 -> x2, blocking collectives: none -> 19.6 us  [norm_back(): lax.psum(jnp.stack([jnp.sum(scaled, axis=-1), jnp.sum(scaled * (centred *...]
    all_gather x2, blocking collectives: 27.2 us -> 38.3 us  [entering(): gathered = jax.tree.map(lambda a: lax.all_gather(a, axis), part)]
    all_gather x2, waiting for transfers between devices: 24.2 us -> 15 us  [entering(): gathered = jax.tree.map(lambda a: lax.all_gather(a, axis), part)]
    dot_general x1, matrix products: 19.7 us -> 10.7 us  [per_device(): jnp.dot(normed_one.T, proj_grad, precision=highest)]
    unnamed x108 -> x115, local copies, waits for them, and re-layouts: 29.6 us -> 26.5 us
  transfers between devices with their start and end apart: 10 -> 11, of which waited for: 8 -> 9; matrix products, arithmetic and copies ran while one was open for 22% -> 17% of each run, Pallas kernels for 0% -> 0%
where the time goes in v1:
time: 819 us; the launch traced here: 811 us
  waiting for transfers between devices  483 us (59%)
  matrix products  129 us (16%)
  blocking collectives  92.6 us (11%)
  local copies, waits for them, and re-layouts  57.1 us (7%)
  other arithmetic  32.5 us (4%)
  between operations  14.7 us (2%)
    psum x1, waiting for transfers between devices, per_device(): lax.psum((gain_attn_share, qkv_weight_grad, out_weight_grad, gain_ffn_sha...  239 us
    reduce_scatter x1, waiting for transfers between devices, per_device(): lax.psum_scatter(branch_out, 'head', scatter_dimension=1, tiled=True)  44.7 us
    all_gather x1, waiting for transfers between devices, per_device(): resid_grad = lax.all_gather(resid_grad_share, 'head', axis=1, tiled=True)  44.1 us
    all_gather x2, blocking collectives, entering(): gathered = jax.tree.map(lambda a: lax.all_gather(a, axis), part)  38.3 us
    reduce_scatter x2, waiting for transfers between devices, norm_back(): lax.psum_scatter(partial_grad, 'head', scatter_dimension=1, tiled=True)  36.1 us
    all_gather x1, waiting for transfers between devices, per_device(): lax.all_gather(tokens, 'head', axis=2, tiled=True)  35.9 us
    all_gather x1, waiting for transfers between devices, per_device(): resid_full = lax.all_gather(resid_share, 'head', axis=1, tiled=True)  34.2 us
    all_gather x1, waiting for transfers between devices, per_device(): grad_full = lax.all_gather(grad_share, 'head', axis=1, tiled=True)  33.3 us
  transfers between devices with their start and end apart: 11, of which 9 were waited for; matrix products, arithmetic and copies ran while one was open for 17% of the time, Pallas kernels for 0%

profile of v1, /device:TPU:0, one launch (start us, length us, event | category | flops | bytes accessed | tf_op | source)
XLA Modules:
  0.0 810.6 jit_solution(9880242845038527068)
XLA Ops:
  8.0 3.5 copy.87
  11.5 9.5 %all-gather.4 = f32[4,1,256]{2,1,0:T(1,128)S(1)} all-gather(f32[1,1,256]{2,1,0:T(1,128)S(1)} %bitcast.167), channel_id=1, replica_groups=mesh['seq'=4,'head'=4,'dp'=2] {'head'}, dimensions={0}, use_global_device_ids=true | all-gather | bytes 5120 | tf_op jit(solution)/shard_map/all_gather | solution.py:112
  21.0 35.9 %all-gather.13.cloned.1.call-done = f32[4,196,1024]{2,0,1:T(4,128)} async-done(((f32[4,196,256]{2,0,1:T(4,128)}), f32[4,196,1024]{2,0,1:T(4,128)}) %all-gather.13.cloned.1.call-update) | async-done | bytes 3211280 | tf_op jit(solution)/shard_map/all_gather | solution.py:111
  57.0 2.4 reduce_sum.132
  59.4 3.0 multiply_reduce_fusion.3
  64.4 6.2 fusion
  70.7 1.7 copy-done.3
  72.4 1.8 fusion.62
  74.3 1.8 fusion.81
  76.1 24.1 %all-gather.1 = f32[16,4,64]{2,1,0:T(4,128)S(1)} all-gather(f32[4,4,64]{2,1,0:T(4,128)S(1)} %fusion.81), channel_id=3, replica_groups=mesh['seq'=4,'head'=4,'dp'=2] {'seq'}, dimensions={0}, use_global_device_ids=true | all-gather | bytes 20480 | tf_op jit(solution)/shard_map/all_gather | solution.py:17
  100.2 5.5 select_reduce_fusion
  105.7 15.0 %all-gather.21.cloned.1.call-done = f32[16,4,64,64]{3,2,1,0:T(8,128)} async-done(((f32[4,4,64,64]{3,2,1,0:T(8,128)}), f32[16,4,64,64]{3,2,1,0:T(8,128)}) %all-gather.21.cloned.1.call-update) | async-done | bytes 1048592 | tf_op jit(solution)/shard_map/all_gather | solution.py:17
  120.8 2.1 fusion.88
  123.0 2.2 fusion.90
  125.8 3.4 broadcast_divide_fusion
  130.6 3.2 fusion.96
  133.8 1.3 copy.82
  136.1 44.7 %reduce-scatter.5.cloned.1.call-done = f32[784,256]{1,0:T(8,128)} async-done(((f32[784,1024]{1,0:T(8,128)}), f32[784,256]{1,0:T(8,128)}) %reduce-scatter.5.cloned.1.call-update) | async-done | bytes 802832 | tf_op jit(solution)/shard_map/reduce_scatter | solution.py:132
  180.8 2.4 add.165
  185.6 8.0 all-gather.5
  193.6 34.2 %all-gather.15.cloned.1.call-done = f32[784,1024]{1,0:T(8,128)} async-done(((f32[784,256]{1,0:T(8,128)}), f32[784,1024]{1,0:T(8,128)}) %all-gather.15.cloned.1.call-update) | async-done | bytes 3211280 | tf_op jit(solution)/shard_map/all_gather | solution.py:135
  227.8 2.1 reduce_sum.139
  229.9 2.6 multiply_reduce_fusion.2
  232.5 1.6 copy-done.5
  234.2 7.0 fusion.10
  241.2 33.3 %all-gather.17.cloned.1.call-done = f32[784,1024]{1,0:T(8,128)} async-done(((f32[784,256]{1,0:T(8,128)}), f32[784,1024]{1,0:T(8,128)}) %all-gather.17.cloned.1.call-update) | async-done | bytes 3211280 | tf_op jit(solution)/shard_map/all_gather | solution.py:143
  274.4 11.0 %fusion.93 = (f32[1024]{0:T(1024)}, f32[784,1024]{1,0:T(8,128)S(1)}) fusion(f32[784,1024]{1,0:T(8,128)} %fusion.10, f32[1024]{0:T(1024)S(1)} %copy-done.49, f32[784,1024]{1,0:T(8,128)} %all-gather.17.cloned.1.call-done, f32[1024,1024]{1,0:T(8,128)} %param.21), kind=kOutput, calls=%fused_computation.132 | convolution fusion | flops 4949359616 | bytes 13836288 | tf_op jit(solution)/shard_map/dot_general | solution.py:146
  285.4 7.5 multiply_reduce_fusion.5
  293.1 9.3 %psum.70 = f32[2,784]{1,0:T(2,128)S(1)} all-reduce(f32[2,784]{1,0:T(2,128)S(1)} %pad_maximum_fusion.1), channel_id=1, replica_groups=mesh['seq'=4,'head'=4,'dp'=2] {'head'}, use_global_device_ids=true, to_apply=%region_13.14 | all-reduce | flops 1568 | bytes 12544 | tf_op jit(solution)/shard_map/psum | solution.py:47
  302.4 35.2 %reduce-scatter.9.cloned.1.call-done = f32[784,256]{1,0:T(8,128)} async-done(((f32[784,1024]{1,0:T(8,128)}), f32[784,256]{1,0:T(8,128)}) %reduce-scatter.9.cloned.1.call-update) | async-done | bytes 802832 | tf_op jit(solution)/shard_map/reduce_scatter | solution.py:54
  337.6 3.2 multiply_reduce_fusion.7
  341.4 44.1 %all-gather.19.cloned.1.call-done = f32[784,1024]{1,0:T(8,128)} async-done(((f32[784,256]{1,0:T(8,128)}), f32[784,1024]{1,0:T(8,128)}) %all-gather.19.cloned.1.call-update) | async-done | bytes 3211280 | tf_op jit(solution)/shard_map/all_gather | solution.py:155
  385.4 3.7 fusion.97
  390.1 3.1 fusion.53
  393.2 10.1 %fusion.51 = f32[784,1024]{1,0:T(8,128)} fusion(f32[1024,1024]{1,0:T(8,128)} %param.21, f32[784,1024]{1,0:T(8,128)} %fusion.10, f32[1024]{0:T(1024)S(1)} %copy-done.49), kind=kOutput, calls=%fused_computation.64 | convolution fusion | flops 4939726848 | bytes 10620928 | tf_op jit(solution)/shard_map/dot_general | solution.py:139
  405.8 5.5 copy.103
  411.2 3.3 reshape.159
  415.6 2.2 fusion.64
  417.9 14.2 %all-gather.3 = f32[16,4,64]{2,1,0:T(4,128)} all-gather(f32[4,4,64]{2,1,0:T(4,128)S(1)} %bitcast.165), channel_id=5, replica_groups=mesh['seq'=4,'head'=4,'dp'=2] {'seq'}, dimensions={0}, use_global_device_ids=true | all-gather | bytes 20480 | tf_op jit(solution)/shard_map/all_gather | solution.py:17
  432.9 1.5 fusion.55
  434.4 2.3 fusion.48
  436.7 3.2 add_bitcast_fusion.1
  440.0 5.9 while.27
  445.9 2.2 fusion.78
  448.1 2.7 add_bitcast_fusion
  450.9 1.9 fusion.43
  453.1 3.7 copy.102
  456.9 5.3 reshape.158
  462.2 11.1 %multiply_reduce_fusion.4 = (f32[784]{0:T(1024)S(1)}, f32[784]{0:T(1024)S(1)}, f32[784,1024]{1,0:T(8,128)}, f32[784,1024]{1,0:T(8,128)}) fusion(f32[1024]{0:T(1024)S(1)} %bitcast.160, f32[784]{0:T(1024)S(1)} %copy-done.38, f32[784,1024]{1,0:T(8,128)} %reshape.159, f32[784]{0:T(1024)S(1)} %copy-done.41, f32[784,768]{0,1:T(8,128)} %reshape.158, ...), kind=kOutput, calls=%fused_computation.21 | convolution fusion | flops 3704191488 | bytes 15204608 | tf_op jit(solution)/shard_map/dot_general | solution.py:168
  474.3 2.9 multiply_multiply_fusion.2
  477.2 3.6 copy.104
  480.8 3.3 reshape.175
  484.1 11.2 %fusion.8 = f32[1024,1024]{1,0:T(8,128)} fusion(f32[784,1024]{1,0:T(8,128)} %copy-done.20, f32[784,1024]{1,0:T(8,128)} %copy-done.5, f32[1024]{0:T(1024)S(1)} %bitcast.164, f32[784]{0:T(1024)S(1)} %add_rsqrt_fusion.1), kind=kOutput, calls=%fused_computation.24 | convolution fusion | flops 4934107136 | bytes 10624064 | tf_op jit(solution)/shard_map/dot_general | solution.py:149
  495.3 9.5 %fusion.50 = f32[1024,1024]{1,0:T(8,128)} fusion(f32[784,1024]{1,0:T(8,128)S(1)} %copy-done.48, f32[784,1024]{1,0:T(8,128)S(1)} %copy-done.51, f32[1024]{0:T(1024)S(1)} %copy-done.50), kind=kOutput, calls=%fused_computation.63 | convolution fusion | flops 4939726848 | bytes 10620928 | tf_op jit(solution)/shard_map/dot_general | solution.py:145
  504.9 3.1 fusion.99
  508.0 10.7 %fusion.98 = f32[1024,3,256]{2,0,1:T(8,128)} fusion(f32[784,1024,1]{1,0,2:T(8,128)S(1)} %copy-done.21, f32[3,256,784]{2,1,0:T(8,128)S(1)} %bitcast.153), kind=kOutput, calls=%fused_computation.135 | convolution fusion | flops 3699376128 | bytes 8765440 | tf_op jit(solution)/shard_map/dot_general | solution.py:166
  522.7 10.2 %psum.71 = f32[2,784]{1,0:T(2,128)S(1)} all-reduce(f32[2,784]{1,0:T(2,128)S(1)} %pad_maximum_fusion.2), channel_id=1, replica_groups=mesh['seq'=4,'head'=4,'dp'=2] {'head'}, use_global_device_ids=true, to_apply=%region_20.21 | all-reduce | flops 1568 | bytes 12544 | tf_op jit(solution)/shard_map/psum | solution.py:47
  533.9 1.8 multiply_reduce_fusion.8
  536.9 17.3 %all-reduce = (f32[256]{0:T(256)}, f32[256]{0:T(256)}, f32[1024]{0:T(1024)}, f32[256]{0:T(256)}) all-reduce(f32[256]{0:T(256)S(1)} %get-tuple-element.218, f32[256]{0:T(256)S(1)} %copy-done.45, f32[1024]{0:T(1024)S(1)} %copy-done.46, f32[256]{0:T(256)S(1)} %reduce_sum.169), channel_id=1, replica_groups=mesh['seq'=4,'head'=4,'dp'=2] {'seq','dp'}, use_global_device_ids=true, to_apply=%region_22.23 | all-reduce | flops 1792 | bytes 14336 | tf_op jit(solution)/shard_map/psum | solution.py:171
  554.2 239.1 %all-reduce.4.cloned.1.call-done = (f32[1024,3,256]{2,0,1:T(8,128)}, f32[256,1024]{1,0:T(8,128)}, f32[1024,1024]{1,0:T(8,128)}, f32[1024,1024]{1,0:T(8,128)}) async-done(((f32[1024,3,256]{2,0,1:T(8,128)}, f32[256,1024]{1,0:T(8,128)}, f32[1024,1024]{1,0:T(8,128)}, f32[1024,1024]{1,0:T(8,128)}), (f32[1024,3,256]{2,0,1:T(8,128)}, f32[256,1024]{1,0:T(8,128)}, f32[1024,1024]{1,0:T(8,128)}, ...) | async-done | bytes 12582928 | tf_op jit(solution)/shard_map/psum | solution.py:171
  793.3 3.9 copy.172
  798.2 2.1 copy.174
  800.3 1.6 copy-done.15
  801.9 2.0 copy.175
  (175 shorter events, 28.2 us)
Async XLA Ops:
  7.2 123.4 %copy-start = (f32[256,1024]{1,0:T(8,128)S(1)}, f32[256,1024]{1,0:T(8,128)}, u32[]{:S(2)}) copy-start(f32[256,1024]{1,0:T(8,128)} %param.17) | copy-start | bytes 3145732
  7.2 49.8 %all-gather.13.cloned.1.call-start = ((), (), s32[]{:S(2)}) async-start(), calls=%async_computation.4 | async-start | bytes 4014080 | tf_op jit(solution)/shard_map/all_gather | solution.py:111
  7.9 3.6 copy-start.43
  7.9 112.8 %all-gather.21.cloned.1.call-start = ((), (), s32[]{:S(2)}) async-start(), calls=%async_computation.12 | async-start | bytes 2621440 | tf_op jit(solution)/shard_map/all_gather | solution.py:17
  59.4 3.1 copy-start.2
  59.4 4.2 copy-start.23
  62.5 1.1 copy-start.26
  62.5 1.9 copy-start.10
  70.7 1.7 copy-start.3
  74.2 106.6 %reduce-scatter.5.cloned.1.call-start = ((), (), s32[]{:S(2)}) async-start(), calls=%async_computation.5 | async-start | bytes 4014080 | tf_op jit(solution)/shard_map/reduce_scatter | solution.py:132
  74.3 51.5 %copy-start.31 = (pred[196,196]{0,1:T(8,128)(4,1)}, pred[196,196]{0,1:T(8,128)(4,1)S(1)}, u32[]{:S(2)}) copy-start(pred[196,196]{0,1:T(8,128)(4,1)S(1)} %iota_compare_fusion) | copy-start | bytes 115252
  120.8 4.9 copy-start.7
  125.7 3.5 copy-start.34
  133.8 94.0 %all-gather.15.cloned.1.call-start = ((), (), s32[]{:S(2)}) async-start(), calls=%async_computation.6 | async-start | bytes 4014080 | tf_op jit(solution)/shard_map/all_gather | solution.py:135
  136.1 49.5 %copy-start.42 = (f32[256]{0:T(256)S(1)}, f32[256]{0:T(256)}, u32[]{:S(2)}) copy-start(f32[256]{0:T(256)} %param.18) | copy-start | bytes 3076
  183.2 91.2 %all-gather.17.cloned.1.call-start = ((), (), s32[]{:S(2)}) async-start(), calls=%async_computation.8 | async-start | bytes 4014080 | tf_op jit(solution)/shard_map/all_gather | solution.py:143
  185.6 152.1 %reduce-scatter.9.cloned.1.call-start = ((), (), s32[]{:S(2)}) async-start(), calls=%async_computation.9 | async-start | bytes 4014080 | tf_op jit(solution)/shard_map/reduce_scatter | solution.py:54
  193.6 91.9 %copy-start.39 = (f32[4,1,256]{2,1,0:T(1,128)}, f32[4,1,256]{2,1,0:T(1,128)S(1)}, u32[]{:S(2)}) copy-start(f32[4,1,256]{2,1,0:T(1,128)S(1)} %all-gather.5) | copy-start | bytes 12292
  229.9 4.2 copy-start.18
  232.5 1.7 copy-start.5
  234.2 40.3 %copy-start.49 = (f32[1024]{0:T(1024)S(1)}, f32[1024]{0:T(1024)}, u32[]{:S(2)}) copy-start(f32[1024]{0:T(1024)} %param.20) | copy-start | bytes 12292
  274.4 11.0 %copy-start.6 = (f32[784,1024]{1,0:T(8,128)S(1)}, f32[784,1024]{1,0:T(8,128)}, u32[]{:S(2)}) copy-start(f32[784,1024]{1,0:T(8,128)} %copy-done.5) | copy-start | bytes 9633796
  274.4 11.0 %copy-start.19 = (f32[1024,1024]{1,0:T(8,128)S(1)}, f32[1024,1024]{1,0:T(8,128)}, u32[]{:S(2)}) copy-start(f32[1024,1024]{1,0:T(8,128)} %param.19) | copy-start | bytes 12582916
  285.4 7.5 copy-start.20
  292.9 44.7 %copy-start.14 = (f32[784,256]{1,0:T(8,128)S(1)}, f32[784,256]{1,0:T(8,128)}, u32[]{:S(2)}) copy-start(f32[784,256]{1,0:T(8,128)} %reshape.156) | copy-start | bytes 2408452
  293.0 92.5 %all-gather.19.cloned.1.call-start = ((), (), s32[]{:S(2)}) async-start(), calls=%async_computation.10 | async-start | bytes 4014080 | tf_op jit(solution)/shard_map/all_gather | solution.py:155
  340.9 49.2 %copy-start.35 = (f32[4,196,4]{1,2,0:T(4,128)S(1)}, f32[4,196,4]{1,2,0:T(4,128)}, u32[]{:S(2)}) copy-start(f32[4,196,4]{1,2,0:T(4,128)} %copy-done.34) | copy-start | bytes 37636
  340.9 99.0 %all-gather.23.cloned.1.call-start = ((), (), s32[]{:S(2)}) async-start(), calls=%async_computation.13 | async-start | bytes 2621440 | tf_op jit(solution)/shard_map/all_gather | solution.py:17
  393.2 126.9 %reduce-scatter.7.cloned.1.call-start = ((), (), s32[]{:S(2)}) async-start(), calls=%async_computation.7 | async-start | bytes 4014080 | tf_op jit(solution)/shard_map/reduce_scatter | solution.py:140
  403.3 0.9 copy-start.24
  403.4 1.0 copy-start.27
  403.4 130.5 %reduce-scatter.11.cloned.1.call-start = ((), (), s32[]{:S(2)}) async-start(), calls=%async_computation.11 | async-start | bytes 4014080 | tf_op jit(solution)/shard_map/reduce_scatter | solution.py:54
  411.2 3.3 copy-start.17
  414.6 17.5 %copy-start.36 = (f32[4,196,4]{1,2,0:T(4,128)S(1)}, f32[4,196,4]{1,2,0:T(4,128)}, u32[]{:S(2)}) copy-start(f32[4,196,4]{1,2,0:T(4,128)} %copy-done.34) | copy-start | bytes 37636
  415.6 17.2 %copy-start.4 = (f32[4,196,3,4,64]{1,4,3,2,0:T(8,128)S(1)}, f32[4,196,3,4,64]{1,4,3,2,0:T(8,128)}, u32[]{:S(2)}) copy-start(f32[4,196,3,4,64]{1,4,3,2,0:T(8,128)} %copy-done.3) | copy-start | bytes 7225348
  432.9 1.6 copy-start.32
  448.1 2.8 copy-start.8
  448.1 2.8 copy-start.33
  448.1 2.8 copy-start.37
  450.9 1.9 copy-start.30
  456.8 5.3 copy-start.38
  456.9 5.3 copy-start.41
  473.3 0.9 copy-start.25
  473.3 1.0 copy-start.28
  473.3 320.0 %all-reduce.4.cloned.1.call-start = ((), (), s32[]{:S(2)}) async-start(), calls=%async_computation.14 | async-start | bytes 25165824 | tf_op jit(solution)/shard_map/psum | solution.py:171
  480.8 3.3 copy-start.40
  484.1 11.2 %copy-start.48 = (f32[784,1024]{1,0:T(8,128)S(1)}, f32[784,1024]{1,0:T(8,128)}, u32[]{:S(2)}) copy-start(f32[784,1024]{1,0:T(8,128)} %all-gather.17.cloned.1.call-done) | copy-start | bytes 9633796
  484.1 11.2 %copy-start.50 = (f32[1024]{0:T(1024)S(1)}, f32[1024]{0:T(1024)}, u32[]{:S(2)}) copy-start(f32[1024]{0:T(1024)} %param.20) | copy-start | bytes 12292
  484.1 11.2 %copy-start.51 = (f32[784,1024]{1,0:T(8,128)S(1)}, f32[784,1024]{1,0:T(8,128)}, u32[]{:S(2)}) copy-start(f32[784,1024]{1,0:T(8,128)} %fusion.10) | copy-start | bytes 9633796
  495.3 9.5 %copy-start.9 = (f32[784,1024]{1,0:T(8,128)S(1)}, f32[784,1024]{1,0:T(8,128)}, u32[]{:S(2)}) copy-start(f32[784,1024]{1,0:T(8,128)} %all-gather.19.cloned.1.call-done) | copy-start | bytes 9633796
  495.3 12.6 %copy-start.21 = (f32[784,1024,1]{1,0,2:T(8,128)S(1)}, f32[784,1024,1]{1,0,2:T(8,128)}, u32[]{:S(2)}) copy-start(f32[784,1024,1]{1,0,2:T(8,128)} %reshape.175) | copy-start | bytes 9633796
  504.8 3.1 copy-start.11
  518.7 1.1 copy-start.22
  518.7 1.4 copy-start.12
  518.7 1.4 copy-start.47
  519.8 14.0 %copy-start.13 = (f32[784,256]{1,0:T(8,128)S(1)}, f32[784,256]{1,0:T(8,128)}, u32[]{:S(2)}) copy-start(f32[784,256]{1,0:T(8,128)} %get-tuple-element.217) | copy-start | bytes 2408452
  519.8 14.0 %copy-start.44 = (f32[256]{0:T(256)S(1)}, f32[256]{0:T(256)}, u32[]{:S(2)}) copy-start(f32[256]{0:T(256)} %param.15) | copy-start | bytes 3076
  533.9 3.1 copy-start.45
  533.9 3.1 copy-start.46
  793.3 3.9 copy-start.29
  793.3 4.9 copy-start.16
  798.2 3.7 copy-start.15
  798.2 5.7 copy-start.1
Sparse Core Ops, SparseCore 0:
  9.9 47.0 all-gather.12
  74.3 46.3 all-gather.20
  133.9 46.8 reduce-scatter.4
  183.3 44.3 all-gather.14
  230.0 44.3 all-gather.16
  293.1 44.5 reduce-scatter.8
  341.0 44.3 all-gather.18
  393.3 46.4 all-gather.22
  442.8 43.1 reduce-scatter.6
  488.9 44.9 reduce-scatter.10
  537.6 255.6 all-reduce.3

commit v2 on v1

--- a/solution.py
+++ b/solution.py
@@ -1,6 +1,10 @@
+import functools
+
 import jax
 import jax.numpy as jnp
 from jax import lax
+from jax.experimental import pallas as pl
+from jax.experimental.pallas import tpu as pltpu
 from jax.sharding import PartitionSpec as P
 
 HEAD_DIM = 64
@@ -193,9 +197,543 @@
     )
 
 
+MESH = pl.DeviceIdType.MESH
+BF = jnp.bfloat16
+F32 = jnp.float32
+LANES = 256
+DIMS = {
+    "nn": (((1,), (0,)), ((), ())),
+    "nt": (((1,), (1,)), ((), ())),
+    "tn": (((0,), (0,)), ((), ())),
+}
+
+
+def round_up(value, step):
+    return -(-value // step) * step
+
+
+def dot(left, right, kind):
+    return lax.dot_general(left, right, DIMS[kind], preferred_element_type=F32)
+
+
+def split(values):
+    high = values.astype(BF)
+    return high, (values - high.astype(F32)).astype(BF)
+
+
+def dot3(left, right, kind):
+    return (
+        dot(left[0], right[0], kind) + dot(left[0], right[1], kind) + dot(left[1], right[0], kind)
+    )
+
+
+def dot2(left, right, kind):
+    return dot(left[0], right, kind) + dot(left[1], right, kind)
+
+
+def lanes(index):
+    if isinstance(index, int):
+        return pl.ds(index * LANES, LANES)
+    return pl.ds(pl.multiple_of(index * LANES, LANES), LANES)
+
+
+def place():
+    z, h, c = lax.axis_index("seq"), lax.axis_index("head"), lax.axis_index("dp")
+    near_x = h + 1 - 2 * lax.rem(h, 2)
+    near_y = lax.rem(h + 2, 4)
+    return z, h, c, near_x, near_y, 3 - h
+
+
+def remote(src, dst, send, recv, device):
+    return pltpu.make_async_remote_copy(
+        src_ref=src, dst_ref=dst, send_sem=send, recv_sem=recv, device_id=device, device_id_type=MESH
+    )
+
+
+def enter(targets):
+    barrier = pltpu.get_barrier_semaphore()
+    for device in targets:
+        pl.semaphore_signal(barrier, inc=1, device_id=device, device_id_type=MESH)
+    pl.semaphore_wait(barrier, len(targets))
+
+
+class Gather:
+    SEMS = 8
+
+    def __init__(self, own, slots, rows, sems):
+        self.own, self.slots, self.sems = own, slots, sems
+        self.half = round_up(rows // 2, 8)
+        self.rows = rows
+
+    def copies(self, i):
+        _, h, _, near_x, near_y, _ = place()
+        slots, sems = self.slots, self.sems
+        first, second = pl.ds(0, self.half), pl.ds(self.half, self.rows - self.half)
+        every = pl.ds(0, self.rows)
+
+        def one(src, dst, place_in, device):
+            return remote(src, dst, sems.at[i, place_in], sems.at[i, 4 + place_in], {"head": device})
+
+        own = self.own(i)
+        return (
+            one(own.at[every], slots.at[i, every, lanes(h)], 0, near_x),
+            one(own.at[every], slots.at[i, every, lanes(h)], 1, near_y),
+            one(slots.at[i, first, lanes(near_x)], slots.at[i, first, lanes(near_x)], 2, near_y),
+            one(slots.at[i, second, lanes(near_y)], slots.at[i, second, lanes(near_y)], 3, near_x),
+        )
+
+    def arrivals(self, i):
+        _, h, _, near_x, near_y, far = place()
+        slots, sems = self.slots, self.sems
+        first, second = pl.ds(0, self.half), pl.ds(self.half, self.rows - self.half)
+        every = pl.ds(0, self.rows)
+
+        def one(dst, place_in, device):
+            return remote(dst, dst, sems.at[i, place_in], sems.at[i, 4 + place_in], {"head": device})
+
+        return (
+            one(slots.at[i, every, lanes(near_x)], 0, near_x),
+            one(slots.at[i, every, lanes(near_y)], 1, near_y),
+            one(slots.at[i, first, lanes(far)], 2, near_y),
+            one(slots.at[i, second, lanes(far)], 3, near_x),
+        )
+
+    def direct(self, i):
+        x, y, _, _ = self.copies(i)
+        x.start()
+        y.start()
+
+    def forward(self, i):
+        x, y, _, _ = self.arrivals(i)
+        x.wait_recv()
+        y.wait_recv()
+        _, _, to_y, to_x = self.copies(i)
+        to_y.start()
+        to_x.start()
+
+    def ready(self, i):
+        _, _, x, y = self.arrivals(i)
+        x.wait_recv()
+        y.wait_recv()
+
+    def finish(self, i):
+        for copy in self.copies(i):
+            copy.wait_send()
+
+
+def head_masks(rows):
+    head = lax.broadcasted_iota(jnp.int32, (rows, LANES), 1) // HEAD_DIM
+    return [head == k for k in range(LANES // HEAD_DIM)]
+
+
+def diagonal_mask():
+    rows = lax.broadcasted_iota(jnp.int32, (LANES, LANES), 0) // HEAD_DIM
+    cols = lax.broadcasted_iota(jnp.int32, (LANES, LANES), 1) // HEAD_DIM
+    return rows == cols
+
+
+def pick(mask, pair):
+    zero = jnp.zeros((), BF)
+    return jnp.where(mask, pair[0], zero), jnp.where(mask, pair[1], zero)
+
+
+def fold(square):
+    square = jnp.where(diagonal_mask(), square, 0.0)
+    return (
+        square[0:HEAD_DIM]
+        + square[HEAD_DIM : 2 * HEAD_DIM]
+        + square[2 * HEAD_DIM : 3 * HEAD_DIM]
+        + square[3 * HEAD_DIM :]
+    )
+
+
+def unfold(wide):
+    return jnp.where(diagonal_mask(), jnp.concatenate([wide] * 4, axis=0), 0.0)
+
+
+def positive(values):
+    return jnp.where(values > 0, values + 1.0, jnp.exp(jnp.minimum(values, 0.0)))
+
+
+def norm_parts(rows):
+    row_mean = jnp.mean(rows, axis=-1, keepdims=True)
+    centred = rows - row_mean
+    row_inv = lax.rsqrt(jnp.mean(centred * centred, axis=-1, keepdims=True) + norm_eps)
+    return centred * row_inv, row_inv
+
+
+def split_rows(source, high, low, rows, step):
+    def one(r, _):
+        s = pl.ds(pl.multiple_of(r * step, step), step)
+        high[s, :], low[s, :] = split(source[s, :])
+        return 0
+
+    lax.fori_loop(0, rows // step, one, 0)
+
+
+STATE = HEAD_DIM + 8
+
+
+def attend_kernel(
+    dims,
+    tok_in, gains_in, wqkv_in, wout_in,
+    tok_out, gains_out, proj_out, den_out, prior_out, mix_out, wout_out,
+    tok, mix, gains, proj, den, prior, state, state_in, wstage, w_h, w_l, n_h, n_l, wout,
+    tok_sem, mix_sem, gain_sem, state_sem, out_sem, pair_sem, load_sem, store_sem,
+):
+    images, length, used, rows = dims
+    width = tok.shape[2]
+    z, h, c, near_x, near_y, far = place()
+    seq = lax.axis_size("seq")
+    out_half = wout_in.shape[0] // 2
+
+    loads = [
+        pltpu.make_async_copy(tok_in.at[i], tok.at[i, :, lanes(h)], load_sem.at[i])
+        for i in range(images)
+    ]
+    loads.append(pltpu.make_async_copy(wqkv_in, wstage, load_sem.at[images]))
+    loads.append(pltpu.make_async_copy(gains_in, gains.at[:, lanes(h)], load_sem.at[images + 1]))
+    for copy in loads:
+        copy.start()
+
+    blank = jnp.zeros((rows - used, LANES), F32)
+    for i in range(images):
+        for other in (near_x, near_y, far):
+            tok[i, used:rows, lanes(other)] = blank
+
+    enter(
+        [{"head": near_x}, {"head": near_y}, {"head": far}, {"dp": 1 - c}]
+        + [{"seq": lax.rem(z + d, seq)} for d in range(1, seq)]
+    )
+    tokens = Gather(lambda i: tok_in.at[i], tok, used, tok_sem)
+    mixes = Gather(lambda i: mix.at[i, :, lanes(h)], mix, used, mix_sem)
+    own_half = pl.ds(pl.multiple_of(c * out_half, out_half), out_half)
+    tokens.direct(0)
+    gain_copies = [
+        remote(gains_in, gains.at[:, lanes(h)], gain_sem.at[k], gain_sem.at[3 + k], {"head": other})
+        for k, other in enumerate((near_x, near_y, far))
+    ]
+    for copy in gain_copies:
+        copy.start()
+    tokens.direct(1)
+    loads[images].wait()
+    split_rows(wstage, w_h, w_l, width, 16)
+    loads[images + 1].wait()
+    for k, other in enumerate((near_x, near_y, far)):
+        remote(
+            gains.at[:, lanes(other)], gains.at[:, lanes(other)], gain_sem.at[k], gain_sem.at[3 + k],
+            {"head": other},
+        ).wait_recv()
+    row_ok = lax.broadcasted_iota(jnp.int32, (rows, LANES), 0) < length
+
+    def project(i):
+        loads[i].wait()
+
+        def normed(r, _):
+            s = pl.ds(pl.multiple_of(r * 16, 16), 16)
+            xhat, _unused = norm_parts(tok[i, s, :])
+            n_h[s, :], n_l[s, :] = split(xhat * gains[0:1, :])
+            return 0
+
+        lax.fori_loop(0, rows // 16, normed, 0)
+
+        def column(k, _):
+            s = lanes(k)
+            proj[i, :, s] = dot3((n_h[...], n_l[...]), (w_h[:, s], w_l[:, s]), "nn")
+            return 0
+
+        lax.fori_loop(0, 3, column, 0)
+        key_feat = jnp.where(row_ok, positive(proj[i, :, lanes(1)]), 0.0)
+        state[i, 0:HEAD_DIM, :] = fold(dot3(split(key_feat), split(proj[i, :, lanes(2)]), "tn"))
+        state[i, HEAD_DIM:, :] = jnp.broadcast_to(
+            jnp.sum(key_feat, axis=0, keepdims=True), (STATE - HEAD_DIM, LANES)
+        )
+        for d in range(1, seq):
+
+            @pl.when(z + d < seq)
+            def _():
+                state_copy(i, d, d).start()
+
+    def state_copy(i, d, step):
+        return remote(
+            state.at[i], state_in.at[d - 1, i], state_sem.at[0, d - 1, i], state_sem.at[1, d - 1, i],
+            {"seq": lax.rem(z + step + seq, seq)},
+        )
+
+    def attend(i):
+        prior[i] = jnp.zeros((STATE, LANES), F32)
+        for d in range(1, seq):
+
+            @pl.when(z >= d)
+            def _():
+                state_copy(i, d, -d).wait_recv()
+                prior[i] = prior[i] + state_in[d - 1, i]
+
+        query_feat = positive(proj[i, :, lanes(0)])
+        key_feat = jnp.where(row_ok, positive(proj[i, :, lanes(1)]), 0.0)
+        query_pair, key_pair = split(query_feat), split(key_feat)
+        value_pair = split(proj[i, :, lanes(2)])
+        total = prior[i, HEAD_DIM : HEAD_DIM + 1, :]
+        ones = jnp.where(diagonal_mask(), 1.0, 0.0).astype(BF)
+        num = dot3(query_pair, split(unfold(prior[i, 0:HEAD_DIM, :])), "nn")
+        below = dot2(split(query_feat * total), ones, "nn")
+        row = lax.broadcasted_iota(jnp.int32, (rows, rows), 0)
+        col = lax.broadcasted_iota(jnp.int32, (rows, rows), 1)
+        for mask in head_masks(rows):
+            scores = dot3(query_pair, pick(mask, key_pair), "nt")
+            score_pair = split(jnp.where(col <= row, scores, 0.0))
+            num = num + dot3(score_pair, pick(mask, value_pair), "nn")
+            below = below + dot2(score_pair, jnp.where(mask, 1.0, 0.0).astype(BF), "nn")
+        den[i] = below
+        mix[i, :, lanes(h)] = jnp.where(row_ok, num / below, 0.0)
+        blank_rows = jnp.zeros((rows - used, LANES), F32)
+        for other in (near_x, near_y, far):
+            mix[i, used:rows, lanes(other)] = blank_rows
+
+    out_copies = [
+        remote(
+            wout_in.at[own_half], wout.at[h, own_half], out_sem.at[0, k], out_sem.at[1, k], {"head": other}
+        )
+        for k, other in enumerate((near_x, near_y, far))
+    ]
+    out_own = pltpu.make_async_copy(wout_in, wout.at[h], load_sem.at[images + 2])
+
+    def out_arrival(k, other):
+        return remote(
+            wout.at[other, own_half], wout.at[other, own_half], out_sem.at[0, k], out_sem.at[1, k],
+            {"head": other},
+        )
+
+    def pair_copy(k, other, which):
+        half = pl.ds(pl.multiple_of(which * out_half, out_half), out_half)
+        return remote(
+            wout.at[other, half], wout.at[other, half], pair_sem.at[0, k], pair_sem.at[1, k],
+            {"dp": 1 - c},
+        )
+
+    peers = tuple(enumerate((near_x, near_y, far)))
+    stores = []
+
+    def store(src, dst):
+        copy = pltpu.make_async_copy(src, dst, store_sem.at[len(stores)])
+        copy.start()
+        stores.append(copy)
+
+    for t in range(images + 2):
+        if t < images:
+            tokens.forward(t)
+            if t + 2 < images:
+                tokens.direct(t + 2)
+            elif t == images - 1:
+                for copy in out_copies:
+                    copy.start()
+                out_own.start()
+        if 1 <= t <= images:
+            tokens.ready(t - 1)
+            project(t - 1)
+            store(tok.at[t - 1], tok_out.at[t - 1])
+            store(proj.at[t - 1], proj_out.at[t - 1])
+        if t >= 2:
+            attend(t - 2)
+            mixes.direct(t - 2)
+            store(den.at[t - 2], den_out.at[t - 2])
+            store(prior.at[t - 2], prior_out.at[t - 2])
+    store(gains, gains_out)
+    out_own.wait()
+    for k, other in peers:
+        out_arrival(k, other).wait_recv()
+        pair_copy(k, other, c).start()
+    for i in range(images):
+        mixes.forward(i)
+    for k, other in peers:
+        pair_copy(k, other, 1 - c).wait_recv()
+    store(wout, wout_out)
+    for i in range(images):
+        mixes.ready(i)
+        store(mix.at[i], mix_out.at[i])
+    for i in range(images):
+        tokens.finish(i)
+        mixes.finish(i)
+        for d in range(1, seq):
+
+            @pl.when(z + d < seq)
+            def _(i=i, d=d):
+                state_copy(i, d, d).wait_send()
+
+    for copy in gain_copies + out_copies:
+        copy.wait_send()
+    for k, other in peers:
+        pair_copy(k, other, c).wait_send()
+    for copy in stores:
+        copy.wait()
+
+
+def attend_call(tokens, gains, wqkv, wout, length):
+    images, rows, _ = tokens.shape
+    used = round_up(length, 8)
+    width = wqkv.shape[0]
+    heads_n = width // LANES
+    dma = pltpu.SemaphoreType.DMA
+    seq = lax.axis_size("seq")
+    any_spec = pl.BlockSpec(memory_space=pl.ANY)
+    shape = lambda *s: jax.ShapeDtypeStruct(s, F32)
+    return pl.pallas_call(
+        functools.partial(attend_kernel, (images, length, used, rows)),
+        out_shape=(
+            shape(images, rows, width),
+            shape(8, width),
+            shape(images, rows, 3 * LANES),
+            shape(images, rows, LANES),
+            shape(images, STATE, LANES),
+            shape(images, rows, width),
+            shape(heads_n, LANES, width),
+        ),
+        in_specs=[any_spec] * 4,
+        out_specs=(any_spec,) * 7,
+        scratch_shapes=[
+            pltpu.VMEM((images, rows, width), F32),
+            pltpu.VMEM((images, rows, width), F32),
+            pltpu.VMEM((8, width), F32),
+            pltpu.VMEM((images, rows, 3 * LANES), F32),
+            pltpu.VMEM((images, rows, LANES), F32),
+            pltpu.VMEM((images, STATE, LANES), F32),
+            pltpu.VMEM((images, STATE, LANES), F32),
+            pltpu.VMEM((seq - 1, images, STATE, LANES), F32),
+            pltpu.VMEM((width, 3 * LANES), F32),
+            pltpu.VMEM((width, 3 * LANES), BF),
+            pltpu.VMEM((width, 3 * LANES), BF),
+            pltpu.VMEM((rows, width), BF),
+            pltpu.VMEM((rows, width), BF),
+            pltpu.VMEM((heads_n, LANES, width), F32),
+            dma((images, Gather.SEMS)),
+            dma((images, Gather.SEMS)),
+            dma((6,)),
+            dma((2, seq - 1, images)),
+            dma((2, 3)),
+            dma((2, 3)),
+            dma((images + 3,)),
+            dma((5 * images + 4,)),
+        ],
+        compiler_params=pltpu.CompilerParams(
+            collective_id=0, has_side_effects=True, vmem_limit_bytes=VMEM_BYTES
+        ),
+    )(tokens, gains, wqkv, wout)
+
+
+VMEM_BYTES = 60 * 1024 * 1024
+
+
+def fast_device(
+    tokens,
+    gain_attn,
+    qkv_weight,
+    out_weight,
+    gain_ffn,
+    up_weight,
+    up_bias,
+    down_weight,
+    down_bias,
+    out_grad,
+):
+    image_count, block_len, local_width = tokens.shape
+    row_count = image_count * block_len
+    model_width = qkv_weight.shape[0]
+    heads_local = local_width // HEAD_DIM
+    rows = round_up(round_up(block_len, 8) + 8, 16)
+    column_start = lax.axis_index("head") * local_width
+    pad = ((0, 0), (0, rows - block_len), (0, 0))
+    proj_weight = qkv_weight.reshape(model_width, 3 * local_width)
+    gains_in = jnp.concatenate([gain_attn[None], gain_ffn[None], jnp.zeros((6, local_width), jnp.float32)])
+    tok, gains, proj, den, prior, mix, wout = attend_call(
+        jnp.pad(tokens, pad), gains_in, proj_weight, out_weight, block_len
+    )
+    gain_first, gain_second = gains[0], gains[1]
+    token_rows = tok[:, :block_len].reshape(row_count, model_width)
+    normed_one = layer_norm(token_rows, gain_first)
+    parts_view = proj[:, :block_len].reshape(image_count, block_len, 3, heads_local, HEAD_DIM)
+    query_proj = parts_view[:, :, 0]
+    key_proj = parts_view[:, :, 1]
+    value_proj = parts_view[:, :, 2]
+    (own_state, own_total), pull_state = jax.vjp(block_state, key_proj, value_proj)
+    zero_pair = (jnp.zeros_like(own_state), jnp.zeros_like(own_total))
+    prior_state = prior[:, :HEAD_DIM].reshape(image_count, HEAD_DIM, heads_local, HEAD_DIM).transpose(0, 2, 1, 3)
+    prior_total = prior[:, HEAD_DIM].reshape(image_count, heads_local, HEAD_DIM)
+    mixed, pull_attend = jax.vjp(
+        block_attend, query_proj, key_proj, value_proj, prior_state, prior_total
+    )
+    mixed_full = mix[:, :block_len].reshape(row_count, model_width)
+    mixed_rows = lax.dynamic_slice_in_dim(mixed_full, column_start, local_width, 1)
+    resid_full = token_rows + jnp.dot(mixed_full, wout.reshape(model_width, model_width), precision=highest)
+    resid_share = lax.dynamic_slice_in_dim(resid_full, column_start, local_width, 1)
+    normed_two = layer_norm(resid_full, gain_second)
+    up_proj = jnp.dot(normed_two, up_weight, precision=highest) + up_bias
+    hidden, pull_act = jax.vjp(mlp_act, up_proj)
+    down_proj = jnp.dot(hidden, down_weight, precision=highest)
+    ffn_share = lax.psum_scatter(down_proj, "head", scatter_dimension=1, tiled=True)
+    output = (resid_share + ffn_share + down_bias).reshape(tokens.shape)
+    grad_share = out_grad.reshape(row_count, local_width)
+    grad_full = lax.all_gather(grad_share, "head", axis=1, tiled=True)
+    down_bias_grad = jnp.sum(grad_share, axis=0)
+    down_weight_grad = jnp.dot(hidden.T, grad_full, precision=highest)
+    hidden_grad = jnp.dot(grad_full, down_weight.T, precision=highest)
+    (up_grad,) = pull_act(hidden_grad)
+    up_bias_grad = jnp.sum(up_grad, axis=0)
+    up_weight_grad = jnp.dot(normed_two.T, up_grad, precision=highest)
+    ffn_grads = lax.psum((up_weight_grad, down_weight_grad), ("seq", "dp"))
+    resid_back, gain_ffn_share = norm_back(
+        jnp.dot(up_grad, up_weight.T, precision=highest), resid_full, gain_second, gain_ffn
+    )
+    resid_grad_share = grad_share + resid_back
+    resid_grad = lax.all_gather(resid_grad_share, "head", axis=1, tiled=True)
+    out_weight_grad = jnp.dot(mixed_rows.T, resid_grad, precision=highest)
+    mixed_grad = jnp.dot(resid_grad, out_weight.T, precision=highest).reshape(mixed.shape)
+    query_grad, key_grad, value_grad, state_grad, total_grad = pull_attend(mixed_grad)
+    later_state, later_total = entering((state_grad, total_grad), "seq", add_pair, zero_pair, True)
+    key_extra, value_extra = pull_state((later_state, later_total))
+    key_grad = key_grad + key_extra
+    value_grad = value_grad + value_extra
+    proj_grad = jnp.stack([query_grad, key_grad, value_grad], axis=2).reshape(
+        row_count, 3 * local_width
+    )
+    qkv_weight_grad = jnp.dot(normed_one.T, proj_grad, precision=highest).reshape(qkv_weight.shape)
+    token_back, gain_attn_share = norm_back(
+        jnp.dot(proj_grad, proj_weight.T, precision=highest), token_rows, gain_first, gain_attn
+    )
+    tokens_grad = (resid_grad_share + token_back).reshape(tokens.shape)
+    summed_grads = lax.psum(
+        (
+            gain_attn_share,
+            qkv_weight_grad,
+            out_weight_grad,
+            gain_ffn_share,
+            up_bias_grad,
+            down_bias_grad,
+        ),
+        ("seq", "dp"),
+    )
+    return (
+        output,
+        tokens_grad,
+        summed_grads[0],
+        summed_grads[1],
+        summed_grads[2],
+        summed_grads[3],
+        ffn_grads[0],
+        summed_grads[4],
+        ffn_grads[1],
+        summed_grads[5],
+    )
+
+
+def device_function(mesh):
+    if mesh.shape["head"] == 4 and mesh.shape["dp"] == 2:
+        return fast_device
+    return per_device
+
+
 def solution(mesh):
     return jax.shard_map(
-        per_device,
+        device_function(mesh),
         mesh=mesh,
         in_specs=(
             P("dp", "seq", "head"),

time: 819 us -> 719 us (0.88)
  waiting for transfers between devices: 483 us -> 310 us
  Pallas kernels: 0 us -> 109 us
  blocking collectives: 92.6 us -> 50.3 us
  local copies, waits for them, and re-layouts: 57.1 us -> 68.4 us
  other arithmetic: 32.5 us -> 21.8 us
    all_gather x4 -> x2, waiting for transfers between devices: 147 us -> 29.2 us  [the longest x1 29.2 us: fast_device(): resid_grad = lax.all_gather(resid_grad_share, 'head', axis=1, tiled=True)]
    pallas_call x0 -> x1, Pallas kernels: none -> 109 us  [attend_call(): pl.pallas_call(functools.partial(attend_kernel, (images, length, used, ro...]
    reduce_scatter x2 -> x1, waiting for transfers between devices: 44.7 us -> 0.01 us  [fast_device(): lax.psum_scatter(down_proj, 'head', scatter_dimension=1, tiled=True)]
    all_gather x2 -> x1, blocking collectives: 38.3 us -> 13.5 us  [entering(): gathered = jax.tree.map(lambda a: lax.all_gather(a, axis), part)]
    all_gather x2 -> x0, blocking collectives: 17.5 us -> none  [the longest x1 9.5 us: per_device(): lax.all_gather(gain_attn, 'head', axis=0, tiled=True)]
    slice x0 -> x6, local copies, waits for them, and re-layouts: none -> 13.4 us  [the longest x2 6.71 us: fast_device(): proj[:, :block_len]]
    all_gather x2 -> x1, waiting for transfers between devices: 15 us -> 1.88 us  [entering(): gathered = jax.tree.map(lambda a: lax.all_gather(a, axis), part)]
    reshape x8 -> x9, local copies, waits for them, and re-layouts: 12.3 us -> 18.8 us  [the longest x1 5.24 us: fast_device(): jnp.stack([query_grad, key_grad, value_grad], axis=2)]
  transfers between devices with their start and end apart: 11 -> 7, of which waited for: 9 -> 5; matrix products, arithmetic and copies ran while one was open for 17% -> 24% of each run, Pallas kernels for 0% -> 15%
where the time goes in v2:
time: 719 us; the launch traced here: 710 us
  waiting for transfers between devices  310 us (43%)
  matrix products  135 us (19%)
  Pallas kernels  109 us (15%)
  local copies, waits for them, and re-layouts  68.4 us (10%)
  blocking collectives  50.3 us (7%)
  other arithmetic  21.8 us (3%)
  between operations  14.9 us (2%)
    psum x1, waiting for transfers between devices, fast_device(): lax.psum((gain_attn_share, qkv_weight_grad, out_weight_grad, gain_ffn_sha...  239 us
    pallas_call x1, Pallas kernels, attend_call(): pl.pallas_call(functools.partial(attend_kernel, (images, length, used, ro...  109 us
    reduce_scatter x2, waiting for transfers between devices, norm_back(): lax.psum_scatter(partial_grad, 'head', scatter_dimension=1, tiled=True)  39.2 us
    all_gather x1, waiting for transfers between devices, fast_device(): resid_grad = lax.all_gather(resid_grad_share, 'head', axis=1, tiled=True)  29.2 us
    unnamed x95, local copies, waits for them, and re-layouts  22.4 us
    psum x2, blocking collectives, norm_back(): lax.psum(jnp.stack([jnp.sum(scaled, axis=-1), jnp.sum(scaled * (centred *...  19.7 us
    psum x1, blocking collectives, fast_device(): lax.psum((gain_attn_share, qkv_weight_grad, out_weight_grad, gain_ffn_sha...  17.2 us
  transfers between devices with their start and end apart: 7, of which 5 were waited for; matrix products, arithmetic and copies ran while one was open for 24% of the time, Pallas kernels for 15%

profile of v2, /device:TPU:0, one launch (start us, length us, event | category | flops | bytes accessed | tf_op | source)
XLA Modules:
  0.0 709.8 jit_solution(14118753292521399517)
XLA Ops:
  7.2 1.4 copy.68
  10.7 2.4 copy.66
  13.1 2.7 copy.67.wqkv_in
  15.8 2.1 pad.4.tok_in
  18.6 109.4 %shard_map.177 = (f32[4,208,1024]{2,1,0:T(8,128)}, f32[8,1024]{1,0:T(8,128)}, f32[4,208,768]{2,1,0:T(8,128)}, f32[4,208,256]{2,1,0:T(8,128)}, f32[4,72,256]{2,1,...) custom-call(f32[4,208,256]{2,1,0:T(8,128)} %pad.4.tok_in, f32[8,256]{1,0:T(8,128)} %maximum_maximum_fusion.gains_in, ...), custom_call_target="tpu_custom_call" | custom-call | tf_op jit(solution)/shard_map/pallas_call | solution.py:580
  128.0 4.1 slice.47
  132.1 3.7 reshape.141
  137.4 3.3 multiply_multiply_fusion.2
  140.7 2.1 reshape.140
  142.8 9.1 %fusion.106 = (f32[784]{0:T(1024)S(1)}, f32[784,1024]{1,0:T(8,128)S(1)}) fusion(f32[784,1024]{1,0:T(8,128)S(1)} %reshape.140, f32[784,1024]{1,0:T(8,128)} %reshape.141, f32[1024,1024]{1,0:T(8,128)} %bitcast.143), kind=kOutput, calls=%fused_computation.141 | convolution fusion | flops 4934106112 | bytes 13831232 | tf_op jit(solution)/shard_map/dot_general | solution.py:666
  152.0 2.1 multiply_reduce_fusion.3
  155.2 1.3 copy-done.15
  156.5 9.0 %fusion.8 = f32[784,1024]{1,0:T(8,128)} fusion(f32[1024,1024]{1,0:T(8,128)S(1)} %copy-done.15, f32[784,1024]{1,0:T(8,128)} %get-tuple-element.169, f32[1024]{0:T(1024)S(1)} %bitcast.148, f32[784]{0:T(1024)S(1)} %add_rsqrt_fusion.1), kind=kOutput, calls=%fused_computation.22 | convolution fusion | flops 4934107136 | bytes 10624064 | tf_op jit(solution)/shard_map/dot_general | solution.py:669
  165.5 10.8 %fusion.102 = (f32[1024]{0:T(1024)}, f32[784,1024]{1,0:T(8,128)S(1)}) fusion(f32[784,1024]{1,0:T(8,128)} %fusion.8, f32[1024]{0:T(1024)S(1)} %copy-done.40, f32[784,1024]{1,0:T(8,128)} %all-gather.6.cloned.1.call-done, f32[1024,1024]{1,0:T(8,128)} %param.19), kind=kOutput, calls=%fused_computation.139 | convolution fusion | flops 4949359616 | bytes 13836288 | tf_op jit(solution)/shard_map/dot_general | solution.py:678
  176.3 9.8 %multiply_reduce_fusion.5 = (f32[784]{0:T(1024)S(1)}, f32[784]{0:T(1024)S(1)}, f32[784,1024]{1,0:T(8,128)}) fusion(f32[1024]{0:T(1024)S(1)} %bitcast.149, f32[784,1024]{1,0:T(8,128)} %get-tuple-element.169, f32[784]{0:T(1024)S(1)} %add_rsqrt_fusion.1, f32[784,1024]{1,0:T(8,128)S(1)} %get-tuple-element.164, f32[1024,1024]{1,0:T(8,128)S(1)} %copy-done.16), kind=kOutput, calls=%fused_computation.18 | convolution fusion | flops 4936514048 | bytes 13841600 | tf_op jit(solution)/shard_map/dot_general | solution.py:684
  186.2 9.2 %psum.70 = f32[2,784]{1,0:T(2,128)S(1)} all-reduce(f32[2,784]{1,0:T(2,128)S(1)} %pad_maximum_fusion.1), channel_id=1, replica_groups=mesh['seq'=4,'head'=4,'dp'=2] {'head'}, use_global_device_ids=true, to_apply=%region_6.7 | all-reduce | flops 1568 | bytes 12544 | tf_op jit(solution)/shard_map/psum | solution.py:51
  195.4 35.3 %reduce-scatter.6.cloned.1.call-done = f32[784,256]{1,0:T(8,128)} async-done(((f32[784,1024]{1,0:T(8,128)}), f32[784,256]{1,0:T(8,128)}) %reduce-scatter.6.cloned.1.call-update) | async-done | bytes 802832 | tf_op jit(solution)/shard_map/reduce_scatter | solution.py:58
  230.7 3.5 multiply_reduce_fusion.6
  235.1 3.3 slice.51
  238.4 3.4 copy.69
  241.9 2.0 fusion.99
  243.9 5.6 select_reduce_fusion
  249.5 29.2 %all-gather.8.cloned.1.call-done = f32[784,1024]{1,0:T(8,128)} async-done(((f32[784,256]{1,0:T(8,128)}), f32[784,1024]{1,0:T(8,128)}) %all-gather.8.cloned.1.call-update) | async-done | bytes 3211280 | tf_op jit(solution)/shard_map/all_gather | solution.py:687
  278.8 5.0 fusion.107
  283.7 3.0 reshape.146
  286.7 1.4 divide_bitcast_fusion
  289.2 3.0 fusion.62
  292.3 10.3 %fusion.55 = f32[784,1024]{1,0:T(8,128)} fusion(f32[1024,1024]{1,0:T(8,128)} %param.19, f32[784,1024]{1,0:T(8,128)} %fusion.8, f32[1024]{0:T(1024)S(1)} %copy-done.40), kind=kOutput, calls=%fused_computation.63 | convolution fusion | flops 4939726848 | bytes 10620928 | tf_op jit(solution)/shard_map/dot_general | solution.py:671
  305.0 1.3 reshape_squeeze.3
  307.4 2.4 fusion.97
  309.8 3.8 fusion.51
  314.5 13.5 %all-gather.1 = f32[16,4,64]{2,1,0:T(4,128)S(1)} all-gather(f32[4,4,64]{2,1,0:T(4,128)S(1)} %bitcast.151), channel_id=3, replica_groups=mesh['seq'=4,'head'=4,'dp'=2] {'seq'}, dimensions={0}, use_global_device_ids=true | all-gather | bytes 20480 | tf_op jit(solution)/shard_map/all_gather | solution.py:21
  328.8 1.5 fusion.60
  330.4 3.2 fusion.49
  333.6 3.3 add_bitcast_fusion.1
  336.9 1.9 all-gather.10.cloned.1.call-done
  339.6 6.4 while.14
  339.6 2.1 bitcast_add_fusion.5
  341.7 2.1 bitcast_add_fusion.5
  343.8 2.1 bitcast_add_fusion.5
  346.1 2.8 fusion.68
  349.0 3.9 fusion.44
  352.8 2.7 add_bitcast_fusion
  355.9 3.7 copy.88
  359.6 5.2 reshape.148
  364.8 10.2 %multiply_reduce_fusion.4 = (f32[784]{0:T(1024)S(1)}, f32[784]{0:T(1024)S(1)}, f32[784,1024]{1,0:T(8,128)}, f32[784,1024]{1,0:T(8,128)}) fusion(f32[1024]{0:T(1024)S(1)} %bitcast.147, f32[784]{0:T(1024)S(1)} %rsqrt.24, f32[784,1024]{1,0:T(8,128)S(1)} %reshape.140, f32[784]{0:T(1024)S(1)} %copy-done.30, f32[784,768]{0,1:T(8,128)} %reshape.148, ...), kind=kOutput, calls=%fused_computation.17 | convolution fusion | flops 3704191488 | bytes 15204608 | tf_op jit(solution)/shard_map/dot_general | solution.py:700
  375.2 4.1 reshape.156
  379.2 10.1 %fusion.6 = f32[1024,1024]{1,0:T(8,128)} fusion(f32[784,1024]{1,0:T(8,128)S(1)} %copy-done.18, f32[784,1024]{1,0:T(8,128)} %get-tuple-element.169, f32[1024]{0:T(1024)S(1)} %bitcast.150, f32[784]{0:T(1024)S(1)} %add_rsqrt_fusion.1), kind=kOutput, calls=%fused_computation.20 | convolution fusion | flops 4934107136 | bytes 10624064 | tf_op jit(solution)/shard_map/dot_general | solution.py:681
  389.4 9.5 %fusion.54 = f32[1024,1024]{1,0:T(8,128)} fusion(f32[784,1024]{1,0:T(8,128)S(1)} %copy-done.39, f32[784,1024]{1,0:T(8,128)S(1)} %copy-done.42, f32[1024]{0:T(1024)S(1)} %copy-done.41), kind=kOutput, calls=%fused_computation.62 | convolution fusion | flops 4939726848 | bytes 10620928 | tf_op jit(solution)/shard_map/dot_general | solution.py:677
  398.9 4.4 fusion.66
  403.4 10.8 %fusion.108 = f32[1024,3,256]{2,0,1:T(8,128)} fusion(f32[784,1024,1]{1,0,2:T(8,128)S(1)} %copy-done.19, f32[3,256,784]{2,1,0:T(8,128)S(1)} %bitcast.140), kind=kOutput, calls=%fused_computation.143 | convolution fusion | flops 3699376128 | bytes 8765440 | tf_op jit(solution)/shard_map/dot_general | solution.py:698
  414.1 1.1 copy-done.20
  415.5 1.5 add_add_fusion
  417.1 1.2 copy.90
  418.3 10.5 %psum.71 = f32[2,784]{1,0:T(2,128)S(1)} all-reduce(f32[2,784]{1,0:T(2,128)S(1)} %pad_maximum_fusion.2), channel_id=1, replica_groups=mesh['seq'=4,'head'=4,'dp'=2] {'head'}, use_global_device_ids=true, to_apply=%region_16.17 | all-reduce | flops 1568 | bytes 12544 | tf_op jit(solution)/shard_map/psum | solution.py:51
  428.9 3.9 reduce-scatter.8.cloned.1.call-done
  432.8 1.8 multiply_reduce_fusion.7
  434.6 1.2 copy.91
  435.8 17.2 %all-reduce.1 = (f32[256]{0:T(256)}, f32[256]{0:T(256)}, f32[1024]{0:T(1024)}, f32[256]{0:T(256)}) all-reduce(f32[256]{0:T(256)S(1)} %get-tuple-element.172, f32[256]{0:T(256)S(1)} %copy-done.33, f32[1024]{0:T(1024)S(1)} %copy-done.37, f32[256]{0:T(256)S(1)} %reduce_sum.159), channel_id=1, replica_groups=mesh['seq'=4,'head'=4,'dp'=2] {'seq','dp'}, use_global_device_ids=true, to_apply=%region_18.19 | all-reduce | flops 1792 | bytes 14336 | tf_op jit(solution)/shard_map/psum | solution.py:703
  453.0 239.2 %all-reduce.5.cloned.1.call-done = (f32[1024,3,256]{2,0,1:T(8,128)}, f32[256,1024]{1,0:T(8,128)}, f32[1024,1024]{1,0:T(8,128)}, f32[1024,1024]{1,0:T(8,128)}) async-done(((f32[1024,3,256]{2,0,1:T(8,128)}, f32[256,1024]{1,0:T(8,128)}, f32[1024,1024]{1,0:T(8,128)}, f32[1024,1024]{1,0:T(8,128)}), (f32[1024,3,256]{2,0,1:T(8,128)}, f32[256,1024]{1,0:T(8,128)}, f32[1024,1024]{1,0:T(8,128)}, ...) | async-done | bytes 12582928 | tf_op jit(solution)/shard_map/psum | solution.py:703
  692.2 3.9 copy.137
  697.1 2.1 copy.139
  699.2 1.6 copy-done.13
  700.8 2.0 copy.140
  (143 shorter events, 15.7 us)
Async XLA Ops:
  7.2 2.5 copy-start.24
  7.2 158.3 %all-gather.6.cloned.1.call-start = ((), (), s32[]{:S(2)}) async-start(), calls=%async_computation.4 | async-start | bytes 4014080 | tf_op jit(solution)/shard_map/all_gather | solution.py:675
  9.6 221.1 %reduce-scatter.6.cloned.1.call-start = ((), (), s32[]{:S(2)}) async-start(), calls=%async_computation.5 | async-start | bytes 4014080 | tf_op jit(solution)/shard_map/reduce_scatter | solution.py:58
  13.1 115.0 %copy-start.1 = (f32[1024,3,256]{0,2,1:T(8,128)}, f32[1024,3,256]{0,2,1:T(8,128)S(1)}, u32[]{:S(2)}) copy-start(f32[1024,3,256]{0,2,1:T(8,128)S(1)} %copy.66) | copy-start | bytes 9437188
  13.1 4.9 copy-start.34
  13.1 4.9 copy-start.35
  132.1 3.7 copy-start
  136.6 4.1 copy-start.27
  137.4 3.3 copy-start.25
  137.4 38.9 %copy-start.31 = (f32[1,1024]{1,0:T(1,128)}, f32[1,1024]{1,0:T(1,128)S(1)}, u32[]{:S(2)}) copy-start(f32[1,1024]{1,0:T(1,128)S(1)} %get-tuple-element.177) | copy-start | bytes 12292
  151.9 3.3 copy-start.7
  152.0 4.5 copy-start.15
  156.5 9.0 %copy-start.40 = (f32[1024]{0:T(1024)S(1)}, f32[1024]{0:T(1024)}, u32[]{:S(2)}) copy-start(f32[1024]{0:T(1024)} %param.18) | copy-start | bytes 12292
  165.5 10.8 %copy-start.16 = (f32[1024,1024]{1,0:T(8,128)S(1)}, f32[1024,1024]{1,0:T(8,128)}, u32[]{:S(2)}) copy-start(f32[1024,1024]{1,0:T(8,128)} %param.17) | copy-start | bytes 12582916
  176.3 9.8 %copy-start.17 = (f32[784,1024]{1,0:T(8,128)}, f32[784,1024]{1,0:T(8,128)S(1)}, u32[]{:S(2)}) copy-start(f32[784,1024]{1,0:T(8,128)S(1)} %get-tuple-element.164) | copy-start | bytes 9633796
  186.1 92.7 %all-gather.8.cloned.1.call-start = ((), (), s32[]{:S(2)}) async-start(), calls=%async_computation.6 | async-start | bytes 4014080 | tf_op jit(solution)/shard_map/all_gather | solution.py:687
  234.2 104.6 %all-gather.10.cloned.1.call-start = ((), (), s32[]{:S(2)}) async-start(), calls=%async_computation.8 | async-start | bytes 2621440 | tf_op jit(solution)/shard_map/all_gather | solution.py:21
  235.0 6.8 copy-start.28
  288.2 1.0 copy-start.3
  292.2 123.3 %reduce-scatter.4.cloned.1.call-start = ((), (), s32[]{:S(2)}) async-start(), calls=%async_computation.3 | async-start | bytes 4014080 | tf_op jit(solution)/shard_map/reduce_scatter | solution.py:672
  302.6 130.2 %reduce-scatter.8.cloned.1.call-start = ((), (), s32[]{:S(2)}) async-start(), calls=%async_computation.7 | async-start | bytes 4014080 | tf_op jit(solution)/shard_map/reduce_scatter | solution.py:58
  307.4 2.4 copy-start.10
  309.8 3.8 copy-start.2
  309.8 18.2 %copy-start.4 = (f32[4,4,64,196]{3,0,2,1:T(4,128)S(1)}, f32[4,4,64,196]{3,0,2,1:T(4,128)}, u32[]{:S(2)}) copy-start(f32[4,4,64,196]{3,0,2,1:T(4,128)} %copy-done.3) | copy-start | bytes 2408452
  309.8 18.2 %copy-start.12 = (f32[4,64,256]{1,2,0:T(8,128)S(1)}, f32[4,64,256]{1,2,0:T(8,128)}, u32[]{:S(2)}) copy-start(f32[4,64,256]{1,2,0:T(8,128)} %copy.105) | copy-start | bytes 786436
  309.8 18.2 %copy-start.29 = (f32[4,4,64]{2,1,0:T(4,128)S(1)}, f32[4,4,64]{2,1,0:T(4,128)}, u32[]{:S(2)}) copy-start(f32[4,4,64]{2,1,0:T(4,128)} %reshape_squeeze.3) | copy-start | bytes 12292
  346.1 2.9 copy-start.5
  348.9 3.9 copy-start.6
  348.9 3.9 copy-start.21
  352.8 2.7 copy-start.23
  359.6 5.2 copy-start.26
  359.6 5.2 copy-start.30
  375.1 317.1 %all-reduce.5.cloned.1.call-start = ((), (), s32[]{:S(2)}) async-start(), calls=%async_computation.9 | async-start | bytes 25165824 | tf_op jit(solution)/shard_map/psum | solution.py:703
  375.1 4.1 copy-start.18
  375.2 4.1 copy-start.32
  379.2 10.2 %copy-start.39 = (f32[784,1024]{1,0:T(8,128)S(1)}, f32[784,1024]{1,0:T(8,128)}, u32[]{:S(2)}) copy-start(f32[784,1024]{1,0:T(8,128)} %all-gather.6.cloned.1.call-done) | copy-start | bytes 9633796
  379.2 10.2 %copy-start.41 = (f32[1024]{0:T(1024)S(1)}, f32[1024]{0:T(1024)}, u32[]{:S(2)}) copy-start(f32[1024]{0:T(1024)} %param.18) | copy-start | bytes 12292
  379.2 10.1 %copy-start.42 = (f32[784,1024]{1,0:T(8,128)S(1)}, f32[784,1024]{1,0:T(8,128)}, u32[]{:S(2)}) copy-start(f32[784,1024]{1,0:T(8,128)} %fusion.8) | copy-start | bytes 9633796
  389.4 9.5 %copy-start.8 = (f32[784,1024]{1,0:T(8,128)S(1)}, f32[784,1024]{1,0:T(8,128)}, u32[]{:S(2)}) copy-start(f32[784,1024]{1,0:T(8,128)} %all-gather.8.cloned.1.call-done) | copy-start | bytes 9633796
  389.4 14.0 %copy-start.19 = (f32[784,1024,1]{1,0,2:T(8,128)S(1)}, f32[784,1024,1]{1,0,2:T(8,128)}, u32[]{:S(2)}) copy-start(f32[784,1024,1]{1,0,2:T(8,128)} %reshape.156) | copy-start | bytes 9633796
  398.9 4.4 copy-start.9
  414.1 1.2 copy-start.20
  414.1 1.4 copy-start.38
  415.3 17.5 %copy-start.11 = (f32[784,256]{1,0:T(8,128)S(1)}, f32[784,256]{1,0:T(8,128)}, u32[]{:S(2)}) copy-start(f32[784,256]{1,0:T(8,128)} %get-tuple-element.171) | copy-start | bytes 2408452
  415.3 17.5 %copy-start.36 = (f32[256]{0:T(256)S(1)}, f32[256]{0:T(256)}, u32[]{:S(2)}) copy-start(f32[256]{0:T(256)} %param.13) | copy-start | bytes 3076
  432.8 3.1 copy-start.33
  432.8 3.1 copy-start.37
  692.2 3.9 copy-start.22
  692.2 4.9 copy-start.14
  697.0 3.7 copy-start.13
Sparse Core Ops, SparseCore 0:
  10.4 73.2 all-gather.5
  186.2 44.4 reduce-scatter.5
  234.3 44.3 all-gather.7
  292.3 46.3 all-gather.9
  341.6 43.2 reduce-scatter.3
  387.8 44.9 reduce-scatter.7
  436.5 255.5 all-reduce.4

commit v3 on v2

--- a/solution.py
+++ b/solution.py
@@ -621,6 +621,400 @@
 
 
 VMEM_BYTES = 60 * 1024 * 1024
+class Scatter:
+    SEMS = 12
+
+    def __init__(self, part, buffers, rows, sems):
+        self.part, self.buffers, self.sems = part, buffers, sems
+        self.half = round_up(rows // 2, 8)
+        self.rows = rows
+        self.first, self.second = pl.ds(0, self.half), pl.ds(self.half, rows - self.half)
+        self.left = pl.ds(0, rows - self.half)
+
+    def slot(self, i, k):
+        rows = self.first if k in (0, 2, 5) else self.left
+        return self.buffers.at[i, k, rows]
+
+    def copy(self, i, k, src, into=None):
+        _, _, _, near_x, near_y, _ = place()
+        into = k if into is None else into
+        device = near_x if into in (0, 2, 4) else near_y
+        return remote(
+            src, self.slot(i, into), self.sems.at[i, into], self.sems.at[i, 6 + into], {"head": device}
+        )
+
+    def sent(self, i):
+        _, _, _, near_x, near_y, far = place()
+        part = self.part(i)
+        return (
+            self.copy(i, 2, part.at[self.first, lanes(far)]),
+            self.copy(i, 3, part.at[self.second, lanes(far)]),
+            self.copy(i, 0, part.at[self.first, lanes(near_x)]),
+            self.copy(i, 1, part.at[self.second, lanes(near_y)]),
+        )
+
+    def passed(self, i):
+        return (
+            self.copy(i, 2, self.slot(i, 2), 5),
+            self.copy(i, 3, self.slot(i, 3), 4),
+        )
+
+    def direct(self, i):
+        for copy in self.sent(i):
+            copy.start()
+
+    def relay(self, i):
+        _, _, _, near_x, near_y, _ = place()
+        part = self.part(i)
+        to_y, to_x = self.passed(i)
+        self.copy(i, 2, self.slot(i, 2)).wait_recv()
+        self.buffers[i, 2, self.first] = self.buffers[i, 2, self.first] + part[self.first, lanes(near_y)]
+        to_y.start()
+        self.copy(i, 3, self.slot(i, 3)).wait_recv()
+        self.buffers[i, 3, self.left] = self.buffers[i, 3, self.left] + part[self.second, lanes(near_x)]
+        to_x.start()
+
+    def total(self, i):
+        _, h, _, _, _, _ = place()
+        part = self.part(i)
+        for k in (0, 5, 1, 4):
+            self.copy(i, k, self.slot(i, k)).wait_recv()
+        first = (
+            part[self.first, lanes(h)] + self.buffers[i, 0, self.first] + self.buffers[i, 5, self.first]
+        )
+        second = part[self.second, lanes(h)] + self.buffers[i, 1, self.left] + self.buffers[i, 4, self.left]
+        return jnp.concatenate([first, second], axis=0)
+
+    def finish(self, i):
+        for copy in self.sent(i) + self.passed(i):
+            copy.wait_send()
+
+
+def activation(values):
+    scale = 0.7978845608028654
+    square = values * values
+    bent = jnp.tanh(scale * values * (1.0 + 0.044715 * square))
+    half = 0.5 * (1.0 + bent)
+    slope = half + 0.5 * values * (1.0 - bent * bent) * (scale * (1.0 + 0.134145 * square))
+    return values * half, slope
+
+
+def to_lanes(first, second, rows):
+    lane = lax.broadcasted_iota(jnp.int32, (rows, 128), 1)
+    both = jnp.where(lane == 0, first, jnp.where(lane == 1, second, 0.0))
+    both = jnp.concatenate([both, jnp.zeros((LANES - rows, 128), F32)], axis=0)
+    return jnp.transpose(both)[0:8]
+
+
+def to_columns(block, rows):
+    tall = jnp.concatenate([block, jnp.zeros((120, LANES), F32)], axis=0)
+    turned = jnp.transpose(tall)[0:rows]
+    return turned[:, 0:1], turned[:, 1:2]
+
+
+def ffn_kernel(
+    dims,
+    tok_in, mix_in, gains_in, wout_in, up_in, bias_in, down_in, down_bias_in, grad_in,
+    out_out, resid_grad_out, down_grad_out, up_grad_out, bias_grad_out, share_grad_out,
+    w_out_h, w_out_l, w_up_h, w_up_l, w_dn_h, w_dn_l, stage, gains, bias, down_bias,
+    grad, tok, mix, pair_h, pair_l, xhat, n_h, n_l, hid_h, hid_l, slope, ug_h, ug_l, g_h, g_l,
+    part_ffn, part_norm, buf_ffn, buf_norm, xhat_own, inv_own, resid_grad, d_down, d_up, d_bias, d_share, out_own,
+    grad_sem, ffn_sem, norm_sem, back_sem, load_sem, stage_sem, image_sem, store_sem,
+):
+    images, length, used, rows = dims
+    width = tok.shape[2]
+    hidden = up_in.shape[1]
+    z, h, c, near_x, near_y, far = place()
+    row_tile = 16
+
+    small = [
+        pltpu.make_async_copy(gains_in, gains, load_sem.at[0]),
+        pltpu.make_async_copy(bias_in, bias, load_sem.at[1]),
+        pltpu.make_async_copy(down_bias_in, down_bias, load_sem.at[2]),
+    ]
+    small += [
+        pltpu.make_async_copy(grad_in.at[i], grad.at[i, :, lanes(h)], load_sem.at[3 + i])
+        for i in range(images)
+    ]
+    depth = stage.shape[1]
+    pieces = []
+    for source, high, low in ((wout_in, w_out_h, w_out_l), (up_in, w_up_h, w_up_l), (down_in, w_dn_h, w_dn_l)):
+        for r in range(source.shape[0] // depth):
+            pieces.append((source.at[pl.ds(r * depth, depth)], high, low, r * depth))
+
+    def piece_copy(k):
+        return pltpu.make_async_copy(pieces[k][0], stage.at[k % 2], stage_sem.at[k % 2])
+
+    def image_copies(i):
+        return (
+            pltpu.make_async_copy(tok_in.at[i], tok.at[i % 2], image_sem.at[0, i % 2]),
+            pltpu.make_async_copy(mix_in.at[i], mix.at[i % 2], image_sem.at[1, i % 2]),
+        )
+
+    piece_copy(0).start()
+    for copy in image_copies(0):
+        copy.start()
+    piece_copy(1).start()
+    for copy in small:
+        copy.start()
+    blank = jnp.zeros((rows - used, LANES), F32)
+    for i in range(images):
+        for other in (near_x, near_y, far):
+            grad[i, used:rows, lanes(other)] = blank
+            resid_grad[i, used:rows, lanes(other)] = blank
+    enter([{"head": near_x}, {"head": near_y}])
+    grads = Gather(lambda i: grad_in.at[i], grad, used, grad_sem)
+    ffn = Scatter(lambda i: part_ffn.at[i % 2], buf_ffn, used, ffn_sem)
+    norm = Scatter(lambda i: part_norm.at[i % 2], buf_norm, rows, norm_sem)
+    back = Gather(lambda i: resid_grad.at[i, :, lanes(h)], resid_grad, used, back_sem)
+    grads.direct(0)
+    grads.direct(1)
+
+    def take(k):
+        piece_copy(k).wait()
+        _, high, low, at = pieces[k]
+
+        def one(r, _):
+            s = pl.ds(pl.multiple_of(r * row_tile, row_tile), row_tile)
+            t = pl.ds(pl.multiple_of(at + r * row_tile, row_tile), row_tile)
+            high[t, :], low[t, :] = split(stage[k % 2, s, :])
+            return 0
+
+        lax.fori_loop(0, depth // row_tile, one, 0)
+        if k + 2 < len(pieces):
+            piece_copy(k + 2).start()
+
+    per = len(pieces) // 3
+    row_ok = lax.broadcasted_iota(jnp.int32, (rows, LANES), 0) < length
+    d_share[...] = jnp.zeros_like(d_share)
+    d_bias[...] = jnp.zeros_like(d_bias)
+    stores = []
+
+    def store(src, dst):
+        copy = pltpu.make_async_copy(src, dst, store_sem.at[len(stores)])
+        copy.start()
+        stores.append(copy)
+
+    def halves(source, high, low):
+        split_rows(source, high, low, rows, row_tile)
+
+    def forward(i):
+        for copy in image_copies(i):
+            copy.wait()
+        if i + 1 < images:
+            for copy in image_copies(i + 1):
+                copy.start()
+        halves(mix.at[i % 2], pair_h, pair_l)
+        if i == 0:
+            for k in range(per):
+                take(k)
+
+        def branch(k, _):
+            s = lanes(k)
+            xhat[:, s] = tok[i % 2, :, s] + dot3(
+                (pair_h[...], pair_l[...]), (w_out_h[:, s], w_out_l[:, s]), "nn"
+            )
+            return 0
+
+        lax.fori_loop(0, width // LANES, branch, 0)
+        out_own[i] = xhat[:, lanes(h)]
+
+        def normed(r, _):
+            s = pl.ds(pl.multiple_of(r * row_tile, row_tile), row_tile)
+            hat, inv = norm_parts(xhat[s, :])
+            xhat[s, :] = hat
+            inv_own[i, s, :] = jnp.broadcast_to(inv, (row_tile, 128))
+            n_h[s, :], n_l[s, :] = split(hat * gains[1:2, :])
+            return 0
+
+        lax.fori_loop(0, rows // row_tile, normed, 0)
+        xhat_own[i] = xhat[:, lanes(h)]
+        if i == 0:
+            for k in range(per, 2 * per):
+                take(k)
+
+        def up(k, _):
+            s = lanes(k)
+            proj = dot3((n_h[...], n_l[...]), (w_up_h[:, s], w_up_l[:, s]), "nn") + bias[0:1, s]
+            act, by = activation(proj)
+            hid_h[:, s], hid_l[:, s] = split(act)
+            slope[:, s] = by
+            return 0
+
+        lax.fori_loop(0, hidden // LANES, up, 0)
+        if i == 0:
+            for k in range(2 * per, 3 * per):
+                take(k)
+        if i >= 2:
+            ffn.finish(i - 2)
+
+        def down(k, _):
+            s = lanes(k)
+            part_ffn[i % 2, :, s] = dot3((hid_h[...], hid_l[...]), (w_dn_h[:, s], w_dn_l[:, s]), "nn")
+            return 0
+
+        lax.fori_loop(0, width // LANES, down, 0)
+
+    def hidden_back(i):
+        halves(grad.at[i], g_h, g_l)
+
+        def one(k, _):
+            s = lanes(k)
+            ug = dot3((g_h[...], g_l[...]), (w_dn_h[s, :], w_dn_l[s, :]), "nt") * slope[:, s]
+            ug_h[:, s], ug_l[:, s] = split(ug)
+            d_bias[0:1, s] = d_bias[0:1, s] + jnp.sum(ug, axis=0, keepdims=True)
+            return 0
+
+        lax.fori_loop(0, hidden // LANES, one, 0)
+
+    def norm_back(i):
+        if i >= 2:
+            norm.finish(i - 2)
+
+        def one(k, sums):
+            s = lanes(k)
+            term = dot3((ug_h[...], ug_l[...]), (w_up_h[s, :], w_up_l[s, :]), "nt")
+            part_norm[i % 2, :, s] = term
+            scaled = term * gains[1:2, s]
+            return (
+                sums[0] + jnp.sum(scaled, axis=-1, keepdims=True),
+                sums[1] + jnp.sum(scaled * xhat[:, s], axis=-1, keepdims=True),
+            )
+
+        none = jnp.zeros((rows, 1), F32)
+        first, second = lax.fori_loop(0, width // LANES, one, (none, none))
+        block = to_lanes(first, second, rows)
+        for k in range(width // LANES):
+            part_norm[i % 2, rows - 8 : rows, lanes(k)] = block
+
+    def weight_grads(i):
+        def one(k, _):
+            s = lanes(k)
+            down = dot3((hid_h[:, s], hid_l[:, s]), (g_h[...], g_l[...]), "tn")
+            up = dot3((n_h[:, s], n_l[:, s]), (ug_h[...], ug_l[...]), "tn")
+            if i == 0:
+                d_down[s, :] = down
+                d_up[s, :] = up
+            else:
+                d_down[s, :] = d_down[s, :] + down
+                d_up[s, :] = d_up[s, :] + up
+            return 0
+
+        lax.fori_loop(0, hidden // LANES, one, 0)
+
+    def output(i):
+        out_own[i, 0:used] = out_own[i, 0:used] + ffn.total(i) + down_bias[0:1, :]
+        store(out_own.at[i], out_out.at[i])
+
+    def resid_back(i):
+        both = norm.total(i)
+        mean, cross = to_columns(both[rows - 8 : rows], rows)
+        own = jnp.where(row_ok, both, 0.0)
+        hat = xhat_own[i]
+        inv = inv_own[i, :, 0:1]
+        scaled = own * gains[1:2, lanes(h)]
+        share = (scaled - mean * (1.0 / width) - hat * (cross * (1.0 / width))) * inv
+        resid_grad[i, :, lanes(h)] = jnp.where(row_ok, grad[i, :, lanes(h)] + share, 0.0)
+        d_share[0:1, :] = d_share[0:1, :] + jnp.sum(own * hat, axis=0, keepdims=True)
+        d_share[1:2, :] = d_share[1:2, :] + jnp.sum(grad[i, :, lanes(h)], axis=0, keepdims=True)
+        back.direct(i)
+
+    for copy in small:
+        copy.wait()
+    for i in range(images):
+        grads.forward(i)
+        if i + 2 < images:
+            grads.direct(i + 2)
+        forward(i)
+        ffn.direct(i)
+        grads.ready(i)
+        hidden_back(i)
+        ffn.relay(i)
+        if i >= 1:
+            norm.relay(i - 1)
+        norm_back(i)
+        norm.direct(i)
+        if i >= 1:
+            resid_back(i - 1)
+        weight_grads(i)
+        output(i)
+        if i >= 1:
+            back.forward(i - 1)
+        if i >= 2:
+            back.ready(i - 2)
+            store(resid_grad.at[i - 2], resid_grad_out.at[i - 2])
+    store(d_down, down_grad_out)
+    store(d_up, up_grad_out)
+    last = images - 1
+    norm.relay(last)
+    resid_back(last)
+    store(d_bias, bias_grad_out)
+    store(d_share, share_grad_out)
+    back.ready(last - 1)
+    store(resid_grad.at[last - 1], resid_grad_out.at[last - 1])
+    back.forward(last)
+    back.ready(last)
+    store(resid_grad.at[last], resid_grad_out.at[last])
+    for i in range(images):
+        grads.finish(i)
+        back.finish(i)
+        if i >= images - 2:
+            ffn.finish(i)
+            norm.finish(i)
+    for copy in stores:
+        copy.wait()
+
+
+def ffn_call(tok, mix, gains, wout, up_weight, up_bias, down_weight, down_bias, grads, length):
+    images, rows, width = tok.shape
+    hidden = up_weight.shape[1]
+    used = round_up(length, 8)
+    dma = pltpu.SemaphoreType.DMA
+    any_spec = pl.BlockSpec(memory_space=pl.ANY)
+    shape = lambda *s: jax.ShapeDtypeStruct(s, F32)
+    vmem = pltpu.VMEM
+    half_used, half_rows = round_up(used // 2, 8), round_up(rows // 2, 8)
+    return pl.pallas_call(
+        functools.partial(ffn_kernel, (images, length, used, rows)),
+        out_shape=(
+            shape(images, rows, LANES),
+            shape(images, rows, width),
+            shape(hidden, width),
+            shape(width, hidden),
+            shape(8, hidden),
+            shape(8, LANES),
+        ),
+        in_specs=[any_spec] * 9,
+        out_specs=(any_spec,) * 6,
+        scratch_shapes=[
+            vmem((width, width), BF), vmem((width, width), BF),
+            vmem((width, hidden), BF), vmem((width, hidden), BF),
+            vmem((hidden, width), BF), vmem((hidden, width), BF),
+            vmem((2, width // 2, width), F32),
+            vmem((8, width), F32), vmem((8, hidden), F32), vmem((8, LANES), F32),
+            vmem((images, rows, width), F32),
+            vmem((2, rows, width), F32), vmem((2, rows, width), F32),
+            vmem((rows, width), BF), vmem((rows, width), BF),
+            vmem((rows, width), F32),
+            vmem((rows, width), BF), vmem((rows, width), BF),
+            vmem((rows, hidden), BF), vmem((rows, hidden), BF),
+            vmem((rows, hidden), F32),
+            vmem((rows, hidden), BF), vmem((rows, hidden), BF),
+            vmem((rows, width), BF), vmem((rows, width), BF),
+            vmem((2, rows, width), F32), vmem((2, rows, width), F32),
+            vmem((images, 6, half_used, LANES), F32), vmem((images, 6, half_rows, LANES), F32),
+            vmem((images, rows, LANES), F32), vmem((images, rows, 128), F32),
+            vmem((images, rows, width), F32),
+            vmem((hidden, width), F32), vmem((width, hidden), F32),
+            vmem((8, hidden), F32), vmem((8, LANES), F32),
+            vmem((images, rows, LANES), F32),
+            dma((images, Gather.SEMS)), dma((images, Scatter.SEMS)), dma((images, Scatter.SEMS)),
+            dma((images, Gather.SEMS)), dma((images + 3,)), dma((2,)), dma((2, 2)), dma((2 * images + 4,)),
+        ],
+        compiler_params=pltpu.CompilerParams(
+            collective_id=1, has_side_effects=True, vmem_limit_bytes=VMEM_BYTES
+        ),
+    )(tok, mix, gains, wout, up_weight, up_bias, down_weight, down_bias, grads)
 
 
 def fast_device(
@@ -647,7 +1041,20 @@
     tok, gains, proj, den, prior, mix, wout = attend_call(
         jnp.pad(tokens, pad), gains_in, proj_weight, out_weight, block_len
     )
-    gain_first, gain_second = gains[0], gains[1]
+    gain_first = gains[0]
+    wide = lambda a: jnp.concatenate([a[None], jnp.zeros((7, a.shape[0]), jnp.float32)])
+    out, resid_grad, down_weight_grad, up_weight_grad, bias_grad, share_grad = ffn_call(
+        tok, mix, gains, wout.reshape(model_width, model_width), up_weight, wide(up_bias), down_weight,
+        wide(down_bias), jnp.pad(out_grad, pad), block_len,
+    )
+    output = out[:, :block_len]
+    up_bias_grad, gain_ffn_share, down_bias_grad = bias_grad[0], share_grad[0], share_grad[1]
+    ffn_grads = lax.psum((up_weight_grad, down_weight_grad), ("seq", "dp"))
+    resid_grad = resid_grad[:, :block_len].reshape(row_count, model_width)
+    resid_grad_share = lax.dynamic_slice_in_dim(resid_grad, column_start, local_width, 1)
+    mixed_rows = lax.dynamic_slice_in_dim(
+        mix[:, :block_len].reshape(row_count, model_width), column_start, local_width, 1
+    )
     token_rows = tok[:, :block_len].reshape(row_count, model_width)
     normed_one = layer_norm(token_rows, gain_first)
     parts_view = proj[:, :block_len].reshape(image_count, block_len, 3, heads_local, HEAD_DIM)
@@ -661,30 +1068,6 @@
     mixed, pull_attend = jax.vjp(
         block_attend, query_proj, key_proj, value_proj, prior_state, prior_total
     )
-    mixed_full = mix[:, :block_len].reshape(row_count, model_width)
-    mixed_rows = lax.dynamic_slice_in_dim(mixed_full, column_start, local_width, 1)
-    resid_full = token_rows + jnp.dot(mixed_full, wout.reshape(model_width, model_width), precision=highest)
-    resid_share = lax.dynamic_slice_in_dim(resid_full, column_start, local_width, 1)
-    normed_two = layer_norm(resid_full, gain_second)
-    up_proj = jnp.dot(normed_two, up_weight, precision=highest) + up_bias
-    hidden, pull_act = jax.vjp(mlp_act, up_proj)
-    down_proj = jnp.dot(hidden, down_weight, precision=highest)
-    ffn_share = lax.psum_scatter(down_proj, "head", scatter_dimension=1, tiled=True)
-    output = (resid_share + ffn_share + down_bias).reshape(tokens.shape)
-    grad_share = out_grad.reshape(row_count, local_width)
-    grad_full = lax.all_gather(grad_share, "head", axis=1, tiled=True)
-    down_bias_grad = jnp.sum(grad_share, axis=0)
-    down_weight_grad = jnp.dot(hidden.T, grad_full, precision=highest)
-    hidden_grad = jnp.dot(grad_full, down_weight.T, precision=highest)
-    (up_grad,) = pull_act(hidden_grad)
-    up_bias_grad = jnp.sum(up_grad, axis=0)
-    up_weight_grad = jnp.dot(normed_two.T, up_grad, precision=highest)
-    ffn_grads = lax.psum((up_weight_grad, down_weight_grad), ("seq", "dp"))
-    resid_back, gain_ffn_share = norm_back(
-        jnp.dot(up_grad, up_weight.T, precision=highest), resid_full, gain_second, gain_ffn
-    )
-    resid_grad_share = grad_share + resid_back
-    resid_grad = lax.all_gather(resid_grad_share, "head", axis=1, tiled=True)
     out_weight_grad = jnp.dot(mixed_rows.T, resid_grad, precision=highest)
     mixed_grad = jnp.dot(resid_grad, out_weight.T, precision=highest).reshape(mixed.shape)
     query_grad, key_grad, value_grad, state_grad, total_grad = pull_attend(mixed_grad)

time: 719 us -> 695 us (0.967)
  Pallas kernels: 109 us -> 216 us
  matrix products: 135 us -> 66.1 us
  waiting for transfers between devices: 310 us -> 273 us
  other arithmetic: 21.8 us -> 10.9 us
  blocking collectives: 50.3 us -> 40.2 us
    pallas_call x0 -> x1, Pallas kernels: none -> 130 us  [ffn_call(): pl.pallas_call(functools.partial(ffn_kernel, (images, length, used, rows)...]
    dot_general x7 -> x0, matrix products: 68.6 us -> none  [the longest x1 10.8 us: fast_device(): hidden_grad = jnp.dot(grad_full, down_weight.T, precision=highest)]
    all_gather x2 -> x0, waiting for transfers between devices: 29.2 us -> none  [the longest x1 29.2 us: fast_device(): resid_grad = lax.all_gather(resid_grad_share, 'head', axis=1, tiled=True)]
    pallas_call x1, Pallas kernels: 109 us -> 86 us  [attend_call(): pl.pallas_call(functools.partial(attend_kernel, (images, length, used, ro...]
    psum x1, waiting for transfers between devices: 239 us -> 225 us  [fast_device(): lax.psum((gain_attn_share, qkv_weight_grad, out_weight_grad, gain_ffn_sha...]
    psum x2 -> x1, blocking collectives: 19.7 us -> 9.33 us  [norm_back(): lax.psum(jnp.stack([jnp.sum(scaled, axis=-1), jnp.sum(scaled * (centred *...]
    reduce_scatter x2 -> x1, waiting for transfers between devices: 39.2 us -> 48.3 us  [norm_back(): lax.psum_scatter(partial_grad, 'head', scatter_dimension=1, tiled=True)]
    unnamed x95 -> x59, local copies, waits for them, and re-layouts: 22.4 us -> 22.8 us
  transfers between devices with their start and end apart: 7 -> 3, of which waited for: 5 -> 2; matrix products, arithmetic and copies ran while one was open for 24% -> 9% of each run, Pallas kernels for 15% -> 0%
where the time goes in v3:
time: 695 us; the launch traced here: 687 us
  waiting for transfers between devices  273 us (39%)
  Pallas kernels  216 us (31%)
  matrix products  66.1 us (10%)
  local copies, waits for them, and re-layouts  65.6 us (9%)
  blocking collectives  40.2 us (6%)
  between operations  14.7 us (2%)
  other arithmetic  10.9 us (2%)
    psum x1, waiting for transfers between devices, fast_device(): lax.psum((gain_attn_share, qkv_weight_grad, out_weight_grad, gain_ffn_sha...  225 us
    pallas_call x1, Pallas kernels, ffn_call(): pl.pallas_call(functools.partial(ffn_kernel, (images, length, used, rows)...  130 us
    pallas_call x1, Pallas kernels, attend_call(): pl.pallas_call(functools.partial(attend_kernel, (images, length, used, ro...  86 us
    reduce_scatter x1, waiting for transfers between devices, norm_back(): lax.psum_scatter(partial_grad, 'head', scatter_dimension=1, tiled=True)  48.3 us
    unnamed x59, local copies, waits for them, and re-layouts  22.8 us
    psum x1, blocking collectives, fast_device(): lax.psum((gain_attn_share, qkv_weight_grad, out_weight_grad, gain_ffn_sha...  17.3 us
  transfers between devices with their start and end apart: 3, of which 2 were waited for; matrix products, arithmetic and copies ran while one was open for 9% of the time, Pallas kernels for 0%

profile of v3, /device:TPU:0, one launch (start us, length us, event | category | flops | bytes accessed | tf_op | source)
XLA Modules:
  0.0 687.1 jit_solution(4806200109803711356)
XLA Ops:
  7.3 2.2 copy.56
  9.4 2.4 copy.57
  11.9 2.7 copy.58.wqkv_in
  14.5 2.1 pad.9.tok_in
  16.7 0.6 concatenate.10.bias_in
  17.9 1.3 copy.59
  19.2 1.0 pad.10.grad_in
  20.3 0.7 maximum_maximum_fusion.gains_in
  20.9 86.0 %shard_map.177 = (f32[4,208,1024]{2,1,0:T(8,128)}, f32[8,1024]{1,0:T(8,128)}, f32[4,208,768]{2,1,0:T(8,128)}, f32[4,208,256]{2,1,0:T(8,128)}, f32[4,72,256]{2,1,...) custom-call(f32[4,208,256]{2,1,0:T(8,128)} %pad.9.tok_in, f32[8,256]{1,0:T(8,128)} %maximum_maximum_fusion.gains_in, ...), custom_call_target="tpu_custom_call" | custom-call | tf_op jit(solution)/shard_map/pallas_call | solution.py:580
  106.9 3.3 slice.52
  110.2 2.4 copy.60
  112.7 0.8 slice_reduce_fusion
  113.5 4.0 select_reduce_fusion
  117.5 0.8 fusion.71
  118.3 129.6 %shard_map.178 = (f32[4,208,256]{2,1,0:T(8,128)}, f32[4,208,1024]{2,1,0:T(8,128)}, f32[1024,1024]{1,0:T(8,128)}, f32[1024,1024]{1,0:T(8,128)}, f32[8,1024]{1,0:T(8,128)}, /*index=5*/f32[8,256]{1,0:T(8,128)}) custom-call(f32[4,208,1024]{2,1,0:T(8,128)} %get-tuple-element.103.tok_in, f32[4,208,1024]{2,1,0:T(8,128)} %get-tuple-element.104.mix_in, ...), custom_call_target="tpu_custom_call" | custom-call | tf_op jit(solution)/shard_map/pallas_call | solution.py:977
  247.9 3.8 fusion
  251.7 0.9 copy-done.5
  252.6 3.5 fusion.65
  256.3 0.8 slice.58
  257.4 0.7 slice.57
  258.7 2.0 copy.89
  260.7 2.5 fusion.69
  263.2 3.6 fusion.37
  266.9 3.5 multiply_multiply_fusion
  270.3 1.7 convolution_add_fusion.1
  272.6 0.9 fusion.52
  273.5 2.0 slice.51
  275.5 1.2 copy-done.9
  276.7 1.9 slice.62
  278.6 3.3 reshape.118
  281.9 3.4 reshape.133
  285.3 3.3 reshape.124
  288.6 13.6 %all-gather.1 = f32[16,4,64]{2,1,0:T(4,128)S(1)} all-gather(f32[4,4,64]{2,1,0:T(4,128)S(1)} %bitcast.150), channel_id=3, replica_groups=mesh['seq'=4,'head'=4,'dp'=2] {'seq'}, dimensions={0}, use_global_device_ids=true | all-gather | bytes 20480 | tf_op jit(solution)/shard_map/all_gather | solution.py:21
  302.2 5.1 fusion.45
  307.3 1.6 fusion.44
  308.9 3.2 fusion.35
  312.1 3.3 add_bitcast_fusion.1
  315.4 3.9 while.14
  315.4 1.2 bitcast_add_fusion.6
  316.7 1.2 bitcast_add_fusion.6
  317.9 1.2 bitcast_add_fusion.6
  319.4 2.3 fusion.47
  321.7 3.8 fusion.30
  325.5 2.7 add_bitcast_fusion
  328.5 2.0 copy.72
  330.6 3.6 reshape.121
  334.2 13.2 %fusion.75 = f32[1024,3,256]{2,0,1:T(8,128)} fusion(f32[784,1024,1]{1,0,2:T(8,128)} %reshape.133, f32[3,256,784]{2,1,0:T(8,128)} %bitcast.140), kind=kOutput, calls=%fused_computation.93 | convolution fusion | flops 3699376128 | bytes 8765440 | tf_op jit(solution)/shard_map/dot_general | solution.py:1081
  347.6 4.1 reshape.122
  351.6 10.4 %multiply_reduce_fusion.2 = (f32[784]{0:T(1024)S(1)}, f32[784]{0:T(1024)S(1)}, f32[784,1024]{1,0:T(8,128)}, f32[784,1024]{1,0:T(8,128)}) fusion(f32[1024]{0:T(1024)S(1)} %bitcast.148, f32[784]{0:T(1024)S(1)} %rsqrt.14, f32[784,1024]{1,0:T(8,128)} %reshape.122, f32[784]{0:T(1024)S(1)} %div.37, f32[784,768]{0,1:T(8,128)} %reshape.121, ...), kind=kOutput, calls=%fused_computation.9 | convolution fusion | flops 3704191488 | bytes 15204608 | tf_op jit(solution)/shard_map/dot_general | solution.py:1083
  362.1 1.2 copy-done.18
  363.3 1.2 copy.74
  364.5 0.8 slice.64
  365.2 0.8 fusion.74
  366.1 9.3 %psum.63 = f32[2,784]{1,0:T(2,128)S(1)} all-reduce(f32[2,784]{1,0:T(2,128)S(1)} %pad_maximum_fusion.1), channel_id=1, replica_groups=mesh['seq'=4,'head'=4,'dp'=2] {'head'}, use_global_device_ids=true, to_apply=%region_9.10 | all-reduce | flops 1568 | bytes 12544 | tf_op jit(solution)/shard_map/psum | solution.py:51
  375.4 225.1 %all-reduce.8.cloned.1.call-done = (f32[1024,3,256]{2,0,1:T(8,128)}, f32[256,1024]{1,0:T(8,128)}, f32[1024,1024]{1,0:T(8,128)}, f32[1024,1024]{1,0:T(8,128)}) async-done(((f32[1024,3,256]{2,0,1:T(8,128)}, f32[256,1024]{1,0:T(8,128)}, f32[1024,1024]{1,0:T(8,128)}, f32[1024,1024]{1,0:T(8,128)}), (f32[1024,3,256]{2,0,1:T(8,128)}, f32[256,1024]{1,0:T(8,128)}, f32[1024,1024]{1,0:T(8,128)}, ...) | async-done | bytes 12582928 | tf_op jit(solution)/shard_map/psum | solution.py:1086
  600.5 48.3 %reduce-scatter.2.cloned.1.call-done = f32[784,256]{1,0:T(8,128)} async-done(((f32[784,1024]{1,0:T(8,128)}), f32[784,256]{1,0:T(8,128)}) %reduce-scatter.2.cloned.1.call-update) | async-done | bytes 802832 | tf_op jit(solution)/shard_map/reduce_scatter | solution.py:58
  648.8 2.0 multiply_reduce_fusion.3
  650.9 1.2 copy.75
  652.1 17.3 %all-reduce.4 = (f32[256]{0:T(256)}, f32[256]{0:T(256)}, f32[1024]{0:T(1024)}, f32[256]{0:T(256)}) all-reduce(f32[256]{0:T(256)S(1)} %get-tuple-element.174, f32[256]{0:T(256)S(1)} %bitcast.155, f32[1024]{0:T(1024)S(1)} %bitcast.149, f32[256]{0:T(256)S(1)} %bitcast.154), channel_id=1, replica_groups=mesh['seq'=4,'head'=4,'dp'=2] {'seq','dp'}, use_global_device_ids=true, to_apply=%region_11.12 | all-reduce | flops 1792 | bytes 14336 | tf_op jit(solution)/shard_map/psum | solution.py:1086
  669.4 3.9 copy.112
  673.3 1.0 copy.113
  674.3 2.1 copy.114
  676.4 1.6 copy-done.11
  678.0 2.0 copy.115
  (80 shorter events, 3.5 us)
Async XLA Ops:
  7.2 308.2 %all-gather.4.cloned.1.call-start = ((), (), s32[]{:S(2)}) async-start(), calls=%async_computation.2 | async-start | bytes 2621440 | tf_op jit(solution)/shard_map/all_gather | solution.py:21
  11.8 4.9 copy-start.1
  11.8 4.8 copy-start.21
  11.8 5.5 copy-start.22
  14.5 5.7 copy-start.20
  14.5 5.7 copy-start.23
  112.6 4.9 copy-start.3
  118.3 129.6 %copy-start.13 = (f32[256,1024]{1,0:T(8,128)S(1)}, f32[256,1024]{1,0:T(8,128)}, u32[]{:S(2)}) copy-start(f32[256,1024]{1,0:T(8,128)} %wout_in.1) | copy-start | bytes 3145732
  251.6 1.0 copy-start.5
  251.6 5.5 copy-start
  256.1 344.4 %all-reduce.8.cloned.1.call-start = ((), (), s32[]{:S(2)}) async-start(), calls=%async_computation.3 | async-start | bytes 25165824 | tf_op jit(solution)/shard_map/psum | solution.py:1086
  256.3 1.1 copy-start.19
  260.7 2.5 copy-start.6
  266.8 3.5 copy-start.14
  266.8 6.7 copy-start.10
  270.3 2.3 copy-start.4
  273.5 3.2 copy-start.9
  288.6 18.7 %copy-start.7 = (f32[4,196,4,64]{1,3,2,0:T(8,128)S(1)}, f32[4,196,4,64]{1,3,2,0:T(8,128)}, u32[]{:S(2)}) copy-start(f32[4,196,4,64]{1,3,2,0:T(8,128)} %copy-done.5) | copy-start | bytes 2408452
  308.9 3.2 copy-start.24
  319.4 2.3 copy-start.8
  321.6 3.8 copy-start.15
  325.5 2.7 copy-start.17
  347.3 301.4 %reduce-scatter.2.cloned.1.call-start = ((), (), s32[]{:S(2)}) async-start(), calls=%async_computation.1 | async-start | bytes 4014080 | tf_op jit(solution)/shard_map/reduce_scatter | solution.py:58
  347.6 4.1 copy-start.2
  362.0 1.2 copy-start.18
  652.1 21.2 %copy-start.16 = (f32[256,1024]{1,0:T(8,128)S(1)}, f32[256,1024]{1,0:T(8,128)}, u32[]{:S(2)}) copy-start(f32[256,1024]{1,0:T(8,128)} %get-tuple-element.267) | copy-start | bytes 3145732
  669.4 4.9 copy-start.12
  674.3 3.7 copy-start.11
Sparse Core Ops, SparseCore 0:
  256.2 45.1 all-gather.3
  347.5 252.9 all-reduce.7
  604.1 44.6 reduce-scatter.1

commit v4 on v3

--- a/solution.py
+++ b/solution.py
@@ -1017,6 +1017,463 @@
     )(tok, mix, gains, wout, up_weight, up_bias, down_weight, down_bias, grads)
 
 
+class Reduce:
+    SEMS = 12
+
+    def __init__(self, slots, sems):
+        self.slots, self.sems = slots, sems
+        self.chunks = []
+
+    def add(self, partial, own, arrived, result, half, rows):
+        c = lax.axis_index("dp")
+        for r in range(half // rows):
+            here = pl.ds(pl.multiple_of(c * half + r * rows, 8), rows)
+            there = pl.ds(pl.multiple_of((1 - c) * half + r * rows, 8), rows)
+            local = pl.ds(r * rows, rows)
+            self.chunks.append(
+                dict(
+                    mine=own(here, local), theirs=partial.at[there], got=arrived.at[local],
+                    result=result.at[here], result_other=result.at[there],
+                    slot=self.slots.at[len(self.chunks), :, pl.ds(0, rows), pl.ds(0, partial.shape[1])],
+                )
+            )
+
+    def side(self, k):
+        z = lax.axis_index("seq")
+        return z if k % 2 == 0 else 3 - z
+
+    def device(self, k, y):
+        return {"seq": y if k % 2 == 0 else 3 - y}
+
+    def sem(self, k, n):
+        return self.sems.at[k, n]
+
+    def pair(self, k):
+        chunk = self.chunks[k]
+        c = lax.axis_index("dp")
+        return remote(chunk["theirs"], chunk["got"], self.sem(k, 0), self.sem(k, 1), {"dp": 1 - c})
+
+    def partial(self, k, into, y):
+        chunk = self.chunks[k]
+        return remote(
+            chunk["mine"], chunk["slot"].at[into], self.sem(k, 2), self.sem(k, 3 + into), self.device(k, y)
+        )
+
+    def outcome(self, k, src, y, send):
+        return remote(src, self.chunks[k]["result"], self.sem(k, send), self.sem(k, 5), self.device(k, y))
+
+    def twin(self, k, src):
+        c = lax.axis_index("dp")
+        return remote(src, self.chunks[k]["result"], self.sem(k, 8), self.sem(k, 9), {"dp": 1 - c})
+
+    def kept(self, k):
+        chunk = self.chunks[k]
+        return pltpu.make_async_copy(chunk["mine"], chunk["result"], self.sem(k, 10))
+
+    def exchange(self, k):
+        self.pair(k).start()
+
+    def combine(self, k):
+        chunk, y = self.chunks[k], self.side(k)
+        self.pair(k).wait_recv()
+        chunk["mine"][...] = chunk["mine"][...] + chunk["got"][...]
+
+        @pl.when(y == 0)
+        def _():
+            self.partial(k, 0, 1).start()
+
+        @pl.when(y == 3)
+        def _():
+            self.partial(k, 0, 2).start()
+
+    def middle(self, k):
+        chunk, y = self.chunks[k], self.side(k)
+
+        @pl.when(y == 2)
+        def _():
+            self.partial(k, 0, 3).wait_recv()
+            chunk["mine"][...] = chunk["mine"][...] + chunk["slot"][0]
+            self.partial(k, 1, 1).start()
+
+    def root(self, k):
+        chunk, y = self.chunks[k], self.side(k)
+
+        @pl.when(y == 1)
+        def _():
+            self.partial(k, 0, 0).wait_recv()
+            self.partial(k, 1, 2).wait_recv()
+            chunk["mine"][...] = chunk["mine"][...] + chunk["slot"][0] + chunk["slot"][1]
+            self.outcome(k, chunk["mine"], 2, 6).start()
+            self.outcome(k, chunk["mine"], 0, 7).start()
+            self.kept(k).start()
+            self.twin(k, chunk["mine"]).start()
+
+    def onward(self, k):
+        chunk, y = self.chunks[k], self.side(k)
+
+        @pl.when(y == 2)
+        def _():
+            self.outcome(k, chunk["result"], 1, 6).wait_recv()
+            self.outcome(k, chunk["result"], 3, 6).start()
+            self.twin(k, chunk["result"]).start()
+
+    def leaf(self, k):
+        chunk, y = self.chunks[k], self.side(k)
+
+        @pl.when(y == 0)
+        def _():
+            self.outcome(k, chunk["result"], 1, 6).wait_recv()
+            self.twin(k, chunk["result"]).start()
+
+        @pl.when(y == 3)
+        def _():
+            self.outcome(k, chunk["result"], 2, 6).wait_recv()
+            self.twin(k, chunk["result"]).start()
+
+    def finish(self, k):
+        chunk, y = self.chunks[k], self.side(k)
+        c = lax.axis_index("dp")
+        self.pair(k).wait_send()
+        remote(
+            chunk["result_other"], chunk["result_other"], self.sem(k, 8), self.sem(k, 9), {"dp": 1 - c}
+        ).wait_recv()
+        self.twin(k, chunk["result"]).wait_send()
+
+        @pl.when(y == 0)
+        def _():
+            self.partial(k, 0, 1).wait_send()
+
+        @pl.when(y == 3)
+        def _():
+            self.partial(k, 0, 2).wait_send()
+
+        @pl.when(y == 2)
+        def _():
+            self.partial(k, 1, 1).wait_send()
+            self.outcome(k, chunk["result"], 3, 6).wait_send()
+
+        @pl.when(y == 1)
+        def _():
+            self.outcome(k, chunk["mine"], 2, 6).wait_send()
+            self.outcome(k, chunk["mine"], 0, 7).wait_send()
+            self.kept(k).wait()
+
+    def tick(self, t):
+        for stage, act in enumerate((self.combine, self.middle, self.root, self.onward, self.leaf)):
+            k = t - LAGS[stage]
+            if 0 <= k < len(self.chunks):
+                act(k)
+
+
+LAGS = (0, 2, 3, 5, 6)
+CHUNK = 64
+
+
+def back_kernel(
+    dims,
+    resid_in, tok_in, gains_in, proj_in, den_in, prior_in, mix_in, wout_in, wqkv_in, down_in, up_in, bias_in, share_in,
+    tok_grad_out, qkv_out, out_out, up_out, down_out, small_out,
+    resid, tok, gains, proj, den, prior, mixed, stage_o, stage_q, wo_h, wo_l, wq_h, wq_l,
+    rg_h, rg_l, n_h, n_l, xhat, pg_h, pg_l, dnum, dden, state, state_in, later,
+    part, buf, xhat_own, inv_own, resid_own, tok_grad, d_out, d_qkv, d_small, d_ffn,
+    got_ffn, got_out, got_qkv, got_small, slots,
+    norm_sem, state_sem, chunk_sem, load_sem, image_sem, ffn_sem, store_sem,
+):
+    images, length, used, rows = dims
+    width = resid.shape[2]
+    z, h, c, near_x, near_y, far = place()
+    seq = lax.axis_size("seq")
+    row_tile = 16
+
+    def first_copies(i):
+        return (
+            pltpu.make_async_copy(resid_in.at[i], resid.at[i % 2], image_sem.at[0, i % 2]),
+            pltpu.make_async_copy(mix_in.at[i, :, lanes(h)], mixed.at[i], load_sem.at[4 + 4 * i]),
+            pltpu.make_async_copy(den_in.at[i], den.at[i], load_sem.at[5 + 4 * i]),
+            pltpu.make_async_copy(proj_in.at[i], proj.at[i], load_sem.at[6 + 4 * i]),
+            pltpu.make_async_copy(prior_in.at[i], prior.at[i], load_sem.at[7 + 4 * i]),
+        )
+
+    def tok_copy(i):
+        return pltpu.make_async_copy(tok_in.at[i], tok.at[i % 2], image_sem.at[1, i % 2])
+
+    weights = (
+        pltpu.make_async_copy(wout_in, stage_o, load_sem.at[0]),
+        pltpu.make_async_copy(wqkv_in, stage_q, load_sem.at[1]),
+        pltpu.make_async_copy(gains_in, gains, load_sem.at[2]),
+    )
+    half = down_in.shape[0] // 2
+    own_rows = pl.ds(pl.multiple_of(c * half, 8), half)
+    ffn_loads = (
+        pltpu.make_async_copy(down_in.at[own_rows], d_ffn.at[0], ffn_sem.at[0]),
+        pltpu.make_async_copy(up_in.at[own_rows], d_ffn.at[1], ffn_sem.at[1]),
+    )
+    small_loads = (
+        pltpu.make_async_copy(bias_in, d_small.at[0:8], load_sem.at[3]),
+        pltpu.make_async_copy(share_in, d_small.at[8:16, lanes(1)], ffn_sem.at[2]),
+    )
+    for copy in first_copies(0) + weights:
+        copy.start()
+    for i in range(1, images):
+        for copy in first_copies(i)[1 if i >= 2 else 0 :]:
+            copy.start()
+    tok_copy(0).start()
+    d_small[...] = jnp.zeros_like(d_small)
+    enter(
+        [{"head": near_x}, {"head": near_y}, {"dp": 1 - c}]
+        + [{"seq": lax.rem(z + d, seq)} for d in range(1, seq)]
+    )
+    reduce = Reduce(slots, chunk_sem)
+    reduce.add(down_in, lambda here, local: d_ffn.at[0, local], got_ffn.at[0], down_out, half, CHUNK)
+    reduce.add(up_in, lambda here, local: d_ffn.at[1, local], got_ffn.at[1], up_out, half, CHUNK)
+    ffn_chunks = len(reduce.chunks)
+    reduce.add(d_out, lambda here, local: d_out.at[here], got_out, out_out, d_out.shape[0] // 2, CHUNK)
+    out_chunks = len(reduce.chunks)
+    reduce.add(d_small, lambda here, local: d_small.at[here], got_small, small_out, 8, 8)
+    reduce.add(d_qkv, lambda here, local: d_qkv.at[here], got_qkv, qkv_out, d_qkv.shape[0] // 2, CHUNK)
+    for k in range(ffn_chunks):
+        reduce.exchange(k)
+    for copy in ffn_loads + small_loads:
+        copy.start()
+    norm = Scatter(lambda i: part.at[i % 2], buf, rows, norm_sem)
+    row_ok = lax.broadcasted_iota(jnp.int32, (rows, LANES), 0) < length
+    clock = [0]
+
+    def tick(times=1):
+        for _ in range(times):
+            reduce.tick(clock[0])
+            clock[0] += 1
+
+    def state_copy(i, d, step):
+        return remote(
+            state.at[i], state_in.at[d - 1, i], state_sem.at[0, d - 1, i], state_sem.at[1, d - 1, i],
+            {"seq": lax.rem(z + step + seq, seq)},
+        )
+
+    def first_half(i):
+        for copy in first_copies(i):
+            copy.wait()
+        split_rows(resid.at[i % 2], rg_h, rg_l, rows, row_tile)
+        resid_own[i] = resid[i % 2, :, lanes(h)]
+        if i + 2 < images:
+            first_copies(i + 2)[0].start()
+        dm = dot3((rg_h[...], rg_l[...]), (wo_h[...], wo_l[...]), "nt")
+        ones = jnp.where(diagonal_mask(), 1.0, 0.0).astype(BF)
+        inverse = 1.0 / den[i]
+        dnum[i] = dm * inverse
+        dden[i] = -dot2(split(dm * mixed[i]), ones, "nn") * inverse
+        query_feat = positive(proj[i, :, lanes(0)])
+        state[i, 0:HEAD_DIM, :] = fold(dot3(split(query_feat), split(dnum[i]), "tn"))
+        state[i, HEAD_DIM:, :] = jnp.broadcast_to(
+            jnp.sum(query_feat * dden[i], axis=0, keepdims=True), (STATE - HEAD_DIM, LANES)
+        )
+        for d in range(1, seq):
+
+            @pl.when(z >= d)
+            def _():
+                state_copy(i, d, -d).start()
+
+        mixed_pair = split(mixed[i])
+
+        def one(k, _):
+            s = lanes(k)
+            term = dot3(mixed_pair, (rg_h[:, s], rg_l[:, s]), "tn")
+            d_out[:, s] = term if i == 0 else d_out[:, s] + term
+            return 0
+
+        lax.fori_loop(0, width // LANES, one, 0)
+
+    def second_half(i):
+        later[...] = jnp.zeros_like(later)
+        for d in range(1, seq):
+
+            @pl.when(z + d < seq)
+            def _():
+                state_copy(i, d, d).wait_recv()
+                later[...] = later[...] + state_in[d - 1, i]
+
+        query, key, value = (proj[i, :, lanes(k)] for k in range(3))
+        query_feat = positive(query)
+        key_feat = jnp.where(row_ok, positive(key), 0.0)
+        query_pair, key_pair, value_pair = split(query_feat), split(key_feat), split(value)
+        dnum_i, dden_i = dnum[i], dden[i]
+        dnum_pair = split(dnum_i)
+        prior_pair = split(unfold(prior[i, 0:HEAD_DIM, :]))
+        later_pair = split(unfold(later[0:HEAD_DIM, :]))
+        fq = dot3(dnum_pair, prior_pair, "nt") + dden_i * prior[i, HEAD_DIM : HEAD_DIM + 1, :]
+        fk = dot3(value_pair, later_pair, "nt") + later[HEAD_DIM : HEAD_DIM + 1, :]
+        fv = dot3(key_pair, later_pair, "nn")
+        row = lax.broadcasted_iota(jnp.int32, (rows, rows), 0)
+        col = lax.broadcasted_iota(jnp.int32, (rows, rows), 1)
+        causal = col <= row
+        for k, mask in enumerate(head_masks(rows)):
+            key_h, query_h = pick(mask, key_pair), pick(mask, query_pair)
+            scores = split(jnp.where(causal, dot3(query_pair, key_h, "nt"), 0.0))
+            pull = dot3(dnum_pair, pick(mask, value_pair), "nt") + dden_i[:, k * HEAD_DIM : k * HEAD_DIM + 1]
+            pull = split(jnp.where(causal, pull, 0.0))
+            fq = fq + dot3(pull, key_h, "nn")
+            fk = fk + dot3(pull, query_h, "tn")
+            fv = fv + dot3(scores, pick(mask, dnum_pair), "tn")
+        slope = lambda v: jnp.where(v > 0, 1.0, jnp.exp(jnp.minimum(v, 0.0)))
+        pg_h[:, lanes(0)], pg_l[:, lanes(0)] = split(fq * slope(query))
+        pg_h[:, lanes(1)], pg_l[:, lanes(1)] = split(jnp.where(row_ok, fk * slope(key), 0.0))
+        pg_h[:, lanes(2)], pg_l[:, lanes(2)] = split(fv)
+
+    def weight_grads(i):
+        tok_copy(i).wait()
+
+        def normed(r, _):
+            s = pl.ds(pl.multiple_of(r * row_tile, row_tile), row_tile)
+            hat, inv = norm_parts(tok[i % 2, s, :])
+            xhat[s, :] = hat
+            inv_own[i, s, :] = jnp.broadcast_to(inv, (row_tile, 128))
+            n_h[s, :], n_l[s, :] = split(hat * gains[0:1, :])
+            return 0
+
+        lax.fori_loop(0, rows // row_tile, normed, 0)
+        xhat_own[i] = xhat[:, lanes(h)]
+        if i + 1 < images:
+            tok_copy(i + 1).start()
+
+        def one(k, _):
+            s = lanes(k)
+            term = dot3((n_h[:, s], n_l[:, s]), (pg_h[...], pg_l[...]), "tn")
+            d_qkv[s, :] = term if i == 0 else d_qkv[s, :] + term
+            return 0
+
+        lax.fori_loop(0, width // LANES, one, 0)
+
+    def norm_back(i):
+        if i >= 2:
+            norm.finish(i - 2)
+
+        def one(k, sums):
+            s = lanes(k)
+            term = dot3((pg_h[...], pg_l[...]), (wq_h[s, :], wq_l[s, :]), "nt")
+            part[i % 2, :, s] = term
+            scaled = term * gains[0:1, s]
+            return (
+                sums[0] + jnp.sum(scaled, axis=-1, keepdims=True),
+                sums[1] + jnp.sum(scaled * xhat[:, s], axis=-1, keepdims=True),
+            )
+
+        none = jnp.zeros((rows, 1), F32)
+        first, second = lax.fori_loop(0, width // LANES, one, (none, none))
+        block = to_lanes(first, second, rows)
+        for k in range(width // LANES):
+            part[i % 2, rows - 8 : rows, lanes(k)] = block
+        norm.direct(i)
+
+    def token_back(i):
+        both = norm.total(i)
+        mean, cross = to_columns(both[rows - 8 : rows], rows)
+        own = jnp.where(row_ok, both, 0.0)
+        hat = xhat_own[i]
+        scaled = own * gains[0:1, lanes(h)]
+        share = (scaled - mean * (1.0 / width) - hat * (cross * (1.0 / width))) * inv_own[i, :, 0:1]
+        tok_grad[i] = resid_own[i] + share
+        d_small[8:9, lanes(0)] = d_small[8:9, lanes(0)] + jnp.sum(own * hat, axis=0, keepdims=True)
+        pltpu.make_async_copy(tok_grad.at[i], tok_grad_out.at[i], store_sem.at[i]).start()
+
+    for copy in weights:
+        copy.wait()
+    split_rows(stage_o, wo_h, wo_l, LANES, row_tile)
+    first_half(0)
+    for copy in ffn_loads:
+        copy.wait()
+    tick()
+    tick()
+    first_half(1)
+    tick()
+    split_rows(stage_q, wq_h, wq_l, width, row_tile)
+    first_half(2)
+    tick()
+    first_half(3)
+    tick()
+    for k in range(ffn_chunks, out_chunks):
+        reduce.exchange(k)
+    for copy in small_loads:
+        copy.wait()
+    d_small[8:9, lanes(2)] = d_small[9:10, lanes(1)]
+    for i in range(images):
+        second_half(i)
+        tick()
+        weight_grads(i)
+        tick()
+        norm_back(i)
+        if i >= 1:
+            token_back(i - 1)
+        norm.relay(i)
+        tick()
+    for k in range(out_chunks + 1, len(reduce.chunks)):
+        reduce.exchange(k)
+    token_back(images - 1)
+    reduce.exchange(out_chunks)
+    while clock[0] < len(reduce.chunks) + LAGS[-1]:
+        tick()
+    for i in range(images):
+        pltpu.make_async_copy(tok_grad.at[i], tok_grad_out.at[i], store_sem.at[i]).wait()
+        if i >= images - 2:
+            norm.finish(i)
+        for d in range(1, seq):
+
+            @pl.when(z >= d)
+            def _(i=i, d=d):
+                state_copy(i, d, -d).wait_send()
+
+    for k in range(len(reduce.chunks)):
+        reduce.finish(k)
+
+
+def back_call(resid, tok, gains, proj, den, prior, mix, wout, wqkv, d_down, d_up, d_bias, d_share, length):
+    images, rows, width = tok.shape
+    hidden = d_down.shape[0]
+    used = round_up(length, 8)
+    dma = pltpu.SemaphoreType.DMA
+    any_spec = pl.BlockSpec(memory_space=pl.ANY)
+    shape = lambda *s: jax.ShapeDtypeStruct(s, F32)
+    vmem = pltpu.VMEM
+    seq = lax.axis_size("seq")
+    chunks = 2 * (hidden // 2 // CHUNK) + LANES // 2 // CHUNK + 1 + width // 2 // CHUNK
+    return pl.pallas_call(
+        functools.partial(back_kernel, (images, length, used, rows)),
+        out_shape=(
+            shape(images, rows, LANES),
+            shape(width, 3 * LANES),
+            shape(LANES, width),
+            shape(width, hidden),
+            shape(hidden, width),
+            shape(16, width),
+        ),
+        in_specs=[any_spec] * 13,
+        out_specs=(any_spec,) * 6,
+        scratch_shapes=[
+            vmem((2, rows, width), F32), vmem((2, rows, width), F32), vmem((8, width), F32),
+            vmem((images, rows, 3 * LANES), F32), vmem((images, rows, LANES), F32), vmem((images, STATE, LANES), F32),
+            vmem((images, rows, LANES), F32),
+            vmem((LANES, width), F32), vmem((width, 3 * LANES), F32),
+            vmem((LANES, width), BF), vmem((LANES, width), BF),
+            vmem((width, 3 * LANES), BF), vmem((width, 3 * LANES), BF),
+            vmem((rows, width), BF), vmem((rows, width), BF), vmem((rows, width), BF), vmem((rows, width), BF),
+            vmem((rows, width), F32), vmem((rows, 3 * LANES), BF), vmem((rows, 3 * LANES), BF),
+            vmem((images, rows, LANES), F32), vmem((images, rows, LANES), F32),
+            vmem((images, STATE, LANES), F32), vmem((seq - 1, images, STATE, LANES), F32), vmem((STATE, LANES), F32),
+            vmem((2, rows, width), F32), vmem((images, 6, round_up(rows // 2, 8), LANES), F32),
+            vmem((images, rows, LANES), F32), vmem((images, rows, 128), F32), vmem((images, rows, LANES), F32),
+            vmem((images, rows, LANES), F32),
+            vmem((LANES, width), F32), vmem((width, 3 * LANES), F32), vmem((16, width), F32),
+            vmem((2, hidden // 2, width), F32), vmem((2, hidden // 2, width), F32),
+            vmem((LANES // 2, width), F32), vmem((width // 2, 3 * LANES), F32), vmem((8, width), F32),
+            vmem((chunks, 2, CHUNK, width), F32),
+            dma((images, Scatter.SEMS)), dma((2, seq - 1, images)), dma((chunks, Reduce.SEMS)),
+            dma((4 + 4 * images,)), dma((2, 2)), dma((3,)), dma((images,)),
+        ],
+        compiler_params=pltpu.CompilerParams(
+            collective_id=2, has_side_effects=True, vmem_limit_bytes=VMEM_BYTES
+        ),
+    )(resid, tok, gains, proj, den, prior, mix, wout, wqkv, d_down, d_up, d_bias, d_share)
+
+
 def fast_device(
     tokens,
     gain_attn,
@@ -1029,82 +1486,38 @@
     down_bias,
     out_grad,
 ):
-    image_count, block_len, local_width = tokens.shape
-    row_count = image_count * block_len
+    block_len, local_width = tokens.shape[1:]
     model_width = qkv_weight.shape[0]
-    heads_local = local_width // HEAD_DIM
     rows = round_up(round_up(block_len, 8) + 8, 16)
-    column_start = lax.axis_index("head") * local_width
     pad = ((0, 0), (0, rows - block_len), (0, 0))
     proj_weight = qkv_weight.reshape(model_width, 3 * local_width)
-    gains_in = jnp.concatenate([gain_attn[None], gain_ffn[None], jnp.zeros((6, local_width), jnp.float32)])
+
+    def wide(*vectors):
+        blank = jnp.zeros((8 - len(vectors), vectors[0].shape[0]), jnp.float32)
+        return jnp.concatenate([v[None] for v in vectors] + [blank])
+
     tok, gains, proj, den, prior, mix, wout = attend_call(
-        jnp.pad(tokens, pad), gains_in, proj_weight, out_weight, block_len
-    )
-    gain_first = gains[0]
-    wide = lambda a: jnp.concatenate([a[None], jnp.zeros((7, a.shape[0]), jnp.float32)])
-    out, resid_grad, down_weight_grad, up_weight_grad, bias_grad, share_grad = ffn_call(
+        jnp.pad(tokens, pad), wide(gain_attn, gain_ffn), proj_weight, out_weight, block_len
+    )
+    out, resid_grad, d_down, d_up, d_bias, d_share = ffn_call(
         tok, mix, gains, wout.reshape(model_width, model_width), up_weight, wide(up_bias), down_weight,
         wide(down_bias), jnp.pad(out_grad, pad), block_len,
     )
-    output = out[:, :block_len]
-    up_bias_grad, gain_ffn_share, down_bias_grad = bias_grad[0], share_grad[0], share_grad[1]
-    ffn_grads = lax.psum((up_weight_grad, down_weight_grad), ("seq", "dp"))
-    resid_grad = resid_grad[:, :block_len].reshape(row_count, model_width)
-    resid_grad_share = lax.dynamic_slice_in_dim(resid_grad, column_start, local_width, 1)
-    mixed_rows = lax.dynamic_slice_in_dim(
-        mix[:, :block_len].reshape(row_count, model_width), column_start, local_width, 1
-    )
-    token_rows = tok[:, :block_len].reshape(row_count, model_width)
-    normed_one = layer_norm(token_rows, gain_first)
-    parts_view = proj[:, :block_len].reshape(image_count, block_len, 3, heads_local, HEAD_DIM)
-    query_proj = parts_view[:, :, 0]
-    key_proj = parts_view[:, :, 1]
-    value_proj = parts_view[:, :, 2]
-    (own_state, own_total), pull_state = jax.vjp(block_state, key_proj, value_proj)
-    zero_pair = (jnp.zeros_like(own_state), jnp.zeros_like(own_total))
-    prior_state = prior[:, :HEAD_DIM].reshape(image_count, HEAD_DIM, heads_local, HEAD_DIM).transpose(0, 2, 1, 3)
-    prior_total = prior[:, HEAD_DIM].reshape(image_count, heads_local, HEAD_DIM)
-    mixed, pull_attend = jax.vjp(
-        block_attend, query_proj, key_proj, value_proj, prior_state, prior_total
-    )
-    out_weight_grad = jnp.dot(mixed_rows.T, resid_grad, precision=highest)
-    mixed_grad = jnp.dot(resid_grad, out_weight.T, precision=highest).reshape(mixed.shape)
-    query_grad, key_grad, value_grad, state_grad, total_grad = pull_attend(mixed_grad)
-    later_state, later_total = entering((state_grad, total_grad), "seq", add_pair, zero_pair, True)
-    key_extra, value_extra = pull_state((later_state, later_total))
-    key_grad = key_grad + key_extra
-    value_grad = value_grad + value_extra
-    proj_grad = jnp.stack([query_grad, key_grad, value_grad], axis=2).reshape(
-        row_count, 3 * local_width
-    )
-    qkv_weight_grad = jnp.dot(normed_one.T, proj_grad, precision=highest).reshape(qkv_weight.shape)
-    token_back, gain_attn_share = norm_back(
-        jnp.dot(proj_grad, proj_weight.T, precision=highest), token_rows, gain_first, gain_attn
-    )
-    tokens_grad = (resid_grad_share + token_back).reshape(tokens.shape)
-    summed_grads = lax.psum(
-        (
-            gain_attn_share,
-            qkv_weight_grad,
-            out_weight_grad,
-            gain_ffn_share,
-            up_bias_grad,
-            down_bias_grad,
-        ),
-        ("seq", "dp"),
+    tok_grad, d_qkv, d_out, d_up, d_down, small = back_call(
+        resid_grad, tok, gains, proj, den, prior, mix, out_weight, proj_weight, d_down, d_up, d_bias, d_share,
+        block_len,
     )
     return (
-        output,
-        tokens_grad,
-        summed_grads[0],
-        summed_grads[1],
-        summed_grads[2],
-        summed_grads[3],
-        ffn_grads[0],
-        summed_grads[4],
-        ffn_grads[1],
-        summed_grads[5],
+        out[:, :block_len],
+        tok_grad[:, :block_len],
+        small[8, 0:LANES],
+        d_qkv.reshape(qkv_weight.shape),
+        d_out,
+        small[8, LANES : 2 * LANES],
+        d_up,
+        small[0],
+        d_down,
+        small[8, 2 * LANES : 3 * LANES],
     )
 
 

time: 695 us -> 444 us (0.64)
  waiting for transfers between devices: 273 us -> 0 us
  Pallas kernels: 216 us -> 402 us
  matrix products: 66.1 us -> 0 us
  blocking collectives: 40.2 us -> 0 us
  local copies, waits for them, and re-layouts: 65.6 us -> 30.9 us
  between operations: 14.7 us -> 1.15 us
  other arithmetic: 10.9 us -> 1.36 us
    psum x1 -> x0, waiting for transfers between devices: 225 us -> none  [fast_device(): lax.psum((gain_attn_share, qkv_weight_grad, out_weight_grad, gain_ffn_sha...]
    pallas_call x0 -> x1, Pallas kernels: none -> 186 us  [back_call(): pl.pallas_call(functools.partial(back_kernel, (images, length, used, rows...]
    dot_general x17 -> x0, matrix products: 66.1 us -> none  [the longest x1 13.2 us: fast_device(): jnp.dot(normed_one.T, proj_grad, precision=highest)]
    reduce_scatter x1 -> x0, waiting for transfers between devices: 48.3 us -> none  [norm_back(): lax.psum_scatter(partial_grad, 'head', scatter_dimension=1, tiled=True)]
    psum x2 -> x0, blocking collectives: 26.6 us -> none  [the longest x1 17.3 us: fast_device(): lax.psum((gain_attn_share, qkv_weight_grad, out_weight_grad, gain_ffn_sha...]
    reshape x6 -> x0, local copies, waits for them, and re-layouts: 16.3 us -> none  [the longest x1 4.08 us: fast_device(): token_rows = tok[:, :block_len].reshape(row_count, model_width)]
    all_gather x1 -> x0, blocking collectives: 13.6 us -> none  [entering(): gathered = jax.tree.map(lambda a: lax.all_gather(a, axis), part)]
    slice x11 -> x4, local copies, waits for them, and re-layouts: 13.6 us -> 5.06 us  [the longest x1 1.35 us: fast_device(): small[0]]
  transfers between devices with their start and end apart: 3 -> 0, of which waited for: 2 -> 0; matrix products, arithmetic and copies ran while one was open for 9% -> 0% of each run, Pallas kernels for 0% -> 0%
where the time goes in v4:
time: 444 us; the launch traced here: 435 us
  Pallas kernels  402 us (91%)
  local copies, waits for them, and re-layouts  30.9 us (7%)
    pallas_call x1, Pallas kernels, back_call(): pl.pallas_call(functools.partial(back_kernel, (images, length, used, rows...  186 us
    pallas_call x1, Pallas kernels, ffn_call(): pl.pallas_call(functools.partial(ffn_kernel, (images, length, used, rows)...  130 us
    pallas_call x1, Pallas kernels, attend_call(): pl.pallas_call(functools.partial(attend_kernel, (images, length, used, ro...  86 us
    unnamed x17, local copies, waits for them, and re-layouts  17.8 us

profile of v4, /device:TPU:0, one launch (start us, length us, event | category | flops | bytes accessed | tf_op | source)
XLA Modules:
  0.0 435.5 jit_solution(4963204609629736517)
XLA Ops:
  0.6 1.3 copy.26
  1.9 1.0 pad.9.tok_in
  2.9 0.1 pad.13.clone
  3.0 1.4 maximum_maximum_fusion.gains_in
  4.4 2.4 copy.27
  6.7 2.4 copy.28.wqkv_in
  9.1 0.0 copy-start.2
  9.1 0.0 copy-start.3
  9.1 0.0 copy-start.1
  9.1 86.0 %shard_map.177 = (f32[4,208,1024]{2,1,0:T(8,128)}, f32[8,1024]{1,0:T(8,128)}, f32[4,208,768]{2,1,0:T(8,128)}, f32[4,208,256]{2,1,0:T(8,128)}, f32[4,72,256]{2,1,...) custom-call(f32[4,208,256]{2,1,0:T(8,128)} %pad.9.tok_in, f32[8,256]{1,0:T(8,128)} %maximum_maximum_fusion.gains_in, ...), custom_call_target="tpu_custom_call" | custom-call | tf_op jit(solution)/shard_map/pallas_call | solution.py:580
  95.1 0.0 copy-done.2
  95.1 0.6 concatenate.10.bias_in
  95.8 0.0 copy-done.3
  95.8 0.6 concatenate.11.down_bias_in
  96.4 0.0 copy-done.1
  96.4 0.2 copy.29
  96.5 1.0 pad.10.grad_in
  97.5 129.8 %shard_map.178 = (f32[4,208,256]{2,1,0:T(8,128)}, f32[4,208,1024]{2,1,0:T(8,128)}, f32[1024,1024]{1,0:T(8,128)}, f32[1024,1024]{1,0:T(8,128)}, f32[8,1024]{1,0:T(8,128)}, /*index=5*/f32[8,256]{1,0:T(8,128)}) custom-call(f32[4,208,1024]{2,1,0:T(8,128)} %get-tuple-element.29.tok_in, f32[4,208,1024]{2,1,0:T(8,128)} %get-tuple-element.30.mix_in, ...), custom_call_target="tpu_custom_call" | custom-call | tf_op jit(solution)/shard_map/pallas_call | solution.py:977
  227.3 1.2 slice.18
  228.5 1.2 copy.32
  229.7 186.3 %shard_map.179 = (f32[4,208,256]{2,1,0:T(8,128)}, f32[1024,768]{1,0:T(8,128)}, f32[256,1024]{1,0:T(8,128)}, f32[1024,1024]{1,0:T(8,128)}, f32[1024,1024]{1,0:T(8,128)}, /*index=5*/f32[16,1024]{1,0:T(8,128)}) custom-call(f32[4,208,1024]{2,1,0:T(8,128)} %get-tuple-element.34.resid_in, f32[4,208,1024]{2,1,0:T(8,128)} %get-tuple-element.29.tok_in, ...), custom_call_target="tpu_custom_call" | custom-call | tf_op jit(solution)/shard_map/pallas_call | solution.py:1438
  416.0 1.2 slice.19
  417.2 1.2 copy.33
  418.4 1.3 fusion
  419.7 2.4 copy.31
  422.1 2.4 copy.34
  424.4 1.4 slice.22
  425.8 2.3 copy.38
  428.1 0.0 copy-start
  428.1 4.9 %copy.39 = f32[1024,1024]{1,0:T(8,128)} copy(f32[1024,1024]{1,0:T(8,128)} %get-tuple-element.87) | data formatting | bytes 8388608
  433.0 0.0 copy-done
  433.0 2.0 copy.40
  (1 shorter events, 0.0 us)
Async XLA Ops:
  9.1 86.0 %copy-start.2 = (f32[1024]{0:T(1024)S(1)}, f32[1024]{0:T(1024)}, u32[]{:S(2)}) copy-start(f32[1024]{0:T(1024)} %param.16) | copy-start | bytes 12292
  9.1 86.7 %copy-start.3 = (f32[256]{0:T(256)S(1)}, f32[256]{0:T(256)}, u32[]{:S(2)}) copy-start(f32[256]{0:T(256)} %param.18) | copy-start | bytes 3076
  9.1 87.3 %copy-start.1 = (f32[4,196,256]{2,0,1:T(4,128)S(1)}, f32[4,196,256]{2,0,1:T(4,128)}, u32[]{:S(2)}) copy-start(f32[4,196,256]{2,0,1:T(4,128)} %param.19) | copy-start | bytes 2408452
  428.1 4.9 %copy-start = (f32[1024,1024]{1,0:T(8,128)S(1)}, f32[1024,1024]{1,0:T(8,128)}, u32[]{:S(2)}) copy-start(f32[1024,1024]{1,0:T(8,128)} %get-tuple-element.89) | copy-start | bytes 12582916
